TPU v7x, 32 devices: a whole 2x2x4 slice. The times are simulated.
32 devices in a mesh: groups: 2 (over y), dom: 8 (over z, x), edge: 2 (over core).
Axes of the slice: x: 2, y: 2, z: 4, core: 2. Of those that a mesh axis runs over, the one named last changes fastest.
Arguments:
- entities: float32 [400, 4096], P(None, ('groups', 'dom')), parts along dimension 1, may hold values from -2.5 to 2.5
- entity_state: float32 [4096], P(('groups', 'dom')), parts along dimension 0, may hold values from 0.1 to 1
- relations: float32 [400, 4096], P(None, 'groups'), parts along dimension 1, may hold values from -4 to 4
- relation_state: float32 [4096], P('groups'), parts along dimension 0, may hold values from 0.1 to 1
- src_rows: int32 [6, 128, 128], P(None, ('groups', 'dom', 'edge')), parts along dimension 1, may hold values from 0 to 255
- rel_ids: int32 [6, 128, 128], P(None, ('groups', 'dom', 'edge')), parts along dimension 1, may hold values from 0 to 2047
- dst_rows: int32 [6, 128, 128], P(None, ('groups', 'dom', 'edge')), parts along dimension 1, may hold values from 0 to 255
- counts: int32 [6, 128], P(None, ('groups', 'dom', 'edge')), parts along dimension 1, may hold values from 1 to 128
- neg_blocks: int32 [6, 128], P(None, ('groups', 'dom', 'edge')), parts along dimension 1, may hold values from 0 to 3
Outputs:
- new_entities: float32 [400, 4096], P(None, ('groups', 'dom')), parts along dimension 1
- new_entity_state: float32 [4096], P(('groups', 'dom')), parts along dimension 0
- new_relations: float32 [400, 4096], P(None, 'groups'), parts along dimension 1
- new_relation_state: float32 [4096], P('groups'), parts along dimension 0
There are 2 independent parts, one for each index of `groups`. A program takes and returns all parts, laid end to end along the dimension named above; each array names one. Nothing has to cross between parts.
All inputs are finite; a program needn't handle non-finite values.
Results may differ from a plain program's by a relative error of at most 0.0024.
Values may be sent and summed in bfloat16 or wider, within the bound.
No kernel may reach another device: no remote copies, remote signals or barrier semaphores. Data moves between devices by JAX's collectives and lax.ppermute only.
A program may use at most 128 MiB of HBM per device.

v0:
```python
import functools

import jax
import jax.numpy as jnp
from jax import lax
from jax.experimental import pallas as pl
from jax.experimental.pallas import tpu as pltpu
from jax.sharding import PartitionSpec as P

learn_rate = 0.1
BF = jnp.bfloat16
F32 = jnp.float32
VMEM_LIMIT = 40 * 1024 * 1024
NN = (((1,), (0,)), ((), ()))
NT = (((1,), (1,)), ((), ()))
TN = (((0,), (0,)), ((), ()))


def mm(a, b, dims=NN):
    return lax.dot_general(a, b, dims, preferred_element_type=F32)


def vmem():
    return pl.BlockSpec(memory_space=pltpu.VMEM)


def smem():
    return pl.BlockSpec(memory_space=pltpu.SMEM)


def anywhere():
    return pl.BlockSpec(memory_space=pl.ANY)


def in_hbm(x):
    return pltpu.with_memory_space_constraint(x, pltpu.HBM)


def cost(flops, size):
    return pl.CostEstimate(flops=flops, bytes_accessed=size, transcendentals=0)


def params():
    return pltpu.CompilerParams(vmem_limit_bytes=VMEM_LIMIT)


def shifted(x, by):
    n = lax.axis_size("dom")
    return lax.ppermute(x, "dom", [(i, (i + by) % n) for i in range(n)])


def beside(x):
    n = lax.axis_size("dom")
    return lax.ppermute(x, "dom", [(i, i ^ 1) for i in range(n)])


def across(x):
    return lax.ppermute(x, "edge", [(0, 1), (1, 0)])


def one_hot(rows_ref, t, count, base):
    blocks, width = rows_ref.shape[1:]
    at = lax.broadcasted_iota(jnp.int32, (count, width), 0)
    idx = rows_ref[t]
    return jnp.concatenate(
        [
            jnp.where(at == base(idx[b : b + 1, :]), 1.0, 0.0).astype(BF)
            for b in range(blocks)
        ],
        axis=1,
    )


def relvec_kernel(t, ids_ref, rel_ref, out_ref):
    rels = rel_ref.shape[1]
    tile = min(rels, 512)
    out = None
    for lo in range(0, rels, tile):
        hot = one_hot(ids_ref, t, tile, lambda i, lo=lo: i - lo)
        part = mm(rel_ref[:, lo : lo + tile], hot)
        out = part if out is None else out + part
    out_ref[...] = out.astype(BF)


def relvec(t, rel_ids, rel16):
    width, rels = rel16.shape
    slots = rel_ids.shape[1] * rel_ids.shape[2]
    return pl.pallas_call(
        functools.partial(relvec_kernel, t),
        in_specs=[vmem()] * 2,
        out_specs=vmem(),
        out_shape=jax.ShapeDtypeStruct((width, slots), BF),
        compiler_params=params(),
        cost_estimate=cost(width * slots, width * slots),
        name="relvec",
    )(rel_ids, rel16)


def relsum_kernel(t, first, ids_ref, drel_ref, *refs):
    step = pl.program_id(0)
    out_ref = refs[-1]
    tile = out_ref.shape[1]
    hot = one_hot(ids_ref, t, tile, lambda i: i - step * tile)
    part = mm(drel_ref[...], hot, NT)
    out_ref[...] = part if first else refs[0][...] + part


def relsum(t, rel_ids, drel, acc, rels):
    width, slots = drel.shape
    tile = min(rels, 512)
    wide = pl.BlockSpec((width, tile), lambda i: (0, i))
    ins = [rel_ids, drel] + ([] if acc is None else [acc])
    return pl.pallas_call(
        functools.partial(relsum_kernel, t, acc is None),
        grid=(rels // tile,),
        in_specs=[
            pl.BlockSpec(rel_ids.shape, lambda i: (0, 0, 0)),
            pl.BlockSpec((width, slots), lambda i: (0, 0)),
        ]
        + ([] if acc is None else [wide]),
        out_specs=wide,
        out_shape=jax.ShapeDtypeStruct((width, rels), F32),
        input_output_aliases={} if acc is None else {2: 0},
        compiler_params=params(),
        cost_estimate=cost(width * slots, width * slots),
        name="relsum",
    )(*ins)


class Limits:
    scratch = lambda shape: [
        pltpu.SMEM((shape[1], shape[0]), jnp.int32),
        pltpu.SMEM((shape[1], shape[0]), jnp.int32),
        pltpu.SemaphoreType.DMA((2,)),
    ]

    def __init__(self, t, from_cnt, from_neg, cnt, neg, sems):
        self.t, self.cnt, self.neg = t, cnt, neg
        self.copies = [
            pltpu.make_async_copy(from_cnt, cnt, sems.at[0]),
            pltpu.make_async_copy(from_neg, neg, sems.at[1]),
        ]
        for copy in self.copies:
            copy.start()

    def wait(self):
        for copy in self.copies:
            copy.wait()

    def count(self, b):
        return self.cnt[b, self.t]

    def negative(self, b):
        return self.neg[b, self.t]


def place():
    dom = lax.axis_index("dom")
    return dom // 2, lax.rem(dom, 2), lax.axis_index("edge")


def localize(edge, half):
    def local(idx):
        moved = idx + edge * half
        return jnp.where(moved >= 2 * half, moved - 2 * half, moved)

    return local


def halves(x):
    hd = x.shape[0] // 2
    return x[:hd], x[hd:]


def make_query(source, rel):
    (s_re, s_im), (w_re, w_im) = halves(source), halves(rel)
    return jnp.concatenate(
        [s_re * w_re - s_im * w_im, s_re * w_im + s_im * w_re], axis=0
    ).astype(BF)


def conj_times(dq, v):
    (dq_re, dq_im), (v_re, v_im) = halves(dq), halves(v)
    return jnp.concatenate(
        [dq_re * v_re + dq_im * v_im, dq_im * v_re - dq_re * v_im], axis=0
    ).astype(BF)


def target_side(shape, limits, query, query_t, target, o_ref, d_ref, w_ref):
    _, blocks, width = shape
    lanes = lambda b: pl.ds(pl.multiple_of(b * width, width), width)
    count = limits.count
    o_ref[...] = target.astype(BF)
    query_f = query.astype(F32)
    pos = jnp.sum(query_f * target, axis=0, keepdims=True)
    lane = lax.broadcasted_iota(jnp.int32, (1, width), 1)
    limits.wait()
    row_i = lax.broadcasted_iota(jnp.int32, (width, width), 0)
    col_j = lax.broadcasted_iota(jnp.int32, (width, width), 1)
    weights = []
    for b in range(blocks):
        nb = limits.negative(b)
        neg = o_ref[:, lanes(nb)]
        at = slice(b * width, (b + 1) * width)
        scores = mm(query[:, at], neg, TN) if query_t is None else mm(query_t[at], neg)
        keep = jnp.logical_and(row_i < count(b), col_j < count(nb))
        weight = jnp.where(keep, jax.nn.sigmoid(scores) / width, 0.0).astype(BF)
        w_ref[:, at] = weight
        weights.append(weight)
    valid = jnp.concatenate(
        [jnp.where(lane < count(b), 1.0, 0.0) for b in range(blocks)], axis=1
    )
    gpos = -jax.nn.sigmoid(-pos) * valid
    d_ref[...] = gpos * query_f
    for b in range(blocks):
        d_ref[:, lanes(limits.negative(b))] += mm(query[:, b * width : (b + 1) * width], weights[b])
    return gpos


def make_dquery(shape, limits, gpos, o_ref, w_ref):
    _, blocks, width = shape
    lanes = lambda b: pl.ds(pl.multiple_of(b * width, width), width)
    out = []
    for b in range(blocks):
        nb = limits.negative(b)
        at = slice(b * width, (b + 1) * width)
        own = gpos[:, at] * o_ref[:, at].astype(F32)
        out.append(own + mm(o_ref[:, lanes(nb)], w_ref[:, at], NT))
    return jnp.concatenate(out, axis=1)


def first_kernel(
    shape, cnt_ref, neg_ref, src_ref, dst_ref, ids_ref, ent_ref, state_ref, rel_ref,
    g_mine, g_other, drel_ref, rel16_ref, ent_mine, state_mine,
    cnt, neg, lim_sems, src, dst, ids, ent, state, rel_buf, o_scr, d_scr, w_scr, in_sems, sems,
):
    rels = rel_buf.shape[1]
    tile = min(rels, 512)
    spans = range(0, rels, tile)
    inputs = [
        pltpu.make_async_copy(there, here, in_sems.at[i])
        for i, (there, here) in enumerate(
            [(src_ref.at[:1], src), (dst_ref.at[:1], dst), (ids_ref.at[:1], ids), (ent_ref, ent), (state_ref, state)]
        )
    ]
    loads = [
        pltpu.make_async_copy(
            rel_ref.at[:, lo : lo + tile], rel_buf.at[:, lo : lo + tile], sems.at[i]
        )
        for i, lo in enumerate(spans)
    ]
    for load in inputs:
        load.start()
    limits = Limits(0, cnt_ref, neg_ref, cnt, neg, lim_sems)
    for load in loads:
        load.start()
    half = ent.shape[1] // 2
    _, _, edge = place()
    local = localize(edge, half)
    inputs[0].wait()
    s_hot = one_hot(src, 0, 2 * half, local)
    inputs[1].wait()
    d_hot = one_hot(dst, 0, 2 * half, local)
    inputs[2].wait()
    ids_hot = [one_hot(ids, 0, tile, lambda i, lo=lo: i - lo) for lo in spans]
    inputs[3].wait()
    inputs[4].wait()
    mine = pl.ds(pl.multiple_of(edge * half, half), half)
    ent_mine[...] = ent[:, mine]
    state_mine[...] = state[:, mine]
    table = jnp.concatenate(
        [ent[:, pl.ds(pl.multiple_of(h * half, half), half)].astype(BF) for h in (edge, 1 - edge)],
        axis=1,
    )
    source = mm(table, s_hot)
    target = mm(table, d_hot)
    rel = None
    for load, lo, hot in zip(loads, spans, ids_hot):
        load.wait()
        low = rel_buf[:, lo : lo + tile].astype(BF)
        rel16_ref[:, lo : lo + tile] = low
        part = mm(low, hot)
        rel = part if rel is None else rel + part
    query = make_query(source, rel)
    gpos = target_side(shape, limits, query, None, target, o_scr, d_scr, w_scr)
    dq = make_dquery(shape, limits, gpos, o_scr, w_scr)
    drel_ref[...] = conj_times(dq, source)
    total = mm(conj_times(dq, rel), s_hot, NT) + mm(d_scr[...].astype(BF), d_hot, NT)
    g_mine[...] = total[:, :half]
    g_other[...] = total[:, half:].astype(BF)


def first_round(cnt, neg, src, dst, rel_ids, entities, state, relations):
    dim, rows = entities.shape
    rels = relations.shape[1]
    _, blocks, width = src.shape
    slots = blocks * width
    sds = jax.ShapeDtypeStruct
    return pl.pallas_call(
        functools.partial(first_kernel, src.shape),
        in_specs=[anywhere()] * 8,
        out_specs=[vmem()] * 6,
        out_shape=[
            sds((dim, rows // 2), F32),
            sds((dim, rows // 2), BF),
            sds((dim, slots), BF),
            sds((dim, rels), BF),
            sds((dim, rows // 2), F32),
            sds((1, rows // 2), F32),
        ],
        scratch_shapes=Limits.scratch(src.shape)
        + [
            pltpu.VMEM((1, blocks, width), jnp.int32),
            pltpu.VMEM((1, blocks, width), jnp.int32),
            pltpu.VMEM((1, blocks, width), jnp.int32),
            pltpu.VMEM((dim, rows), F32),
            pltpu.VMEM((1, rows), F32),
            pltpu.VMEM((dim, rels), F32),
            pltpu.VMEM((dim, slots), BF),
            pltpu.VMEM((dim, slots), F32),
            pltpu.VMEM((width, slots), BF),
            pltpu.SemaphoreType.DMA((5,)),
            pltpu.SemaphoreType.DMA((-(-rels // min(rels, 512)),)),
        ],
        compiler_params=params(),
        cost_estimate=cost(2 * dim * slots * (rels + 4 * rows), 8 * dim * rels),
        name="first_round",
    )(*(in_hbm(x) for x in (cnt, neg, src, dst, rel_ids, entities, state, relations)))


def source_kernel(
    t, src_ref, dst_ref, own0, own1, rel_ref,
    query_ref, query_t_ref, source_ref, s_hot_ref, d_hot_ref, d_hot_t_ref,
):
    half = own0.shape[1]
    local = localize(place()[2], half)
    s_hot = one_hot(src_ref, t, 2 * half, local)
    d_hot = one_hot(dst_ref, t, 2 * half, local)
    s_hot_ref[...] = s_hot
    d_hot_ref[...] = d_hot
    d_hot_t_ref[...] = d_hot.T
    source = mm(jnp.concatenate([own0[...], own1[...]], axis=1), s_hot)
    source_ref[...] = source.astype(BF)
    query = make_query(source, rel_ref[...].astype(F32))
    query_ref[...] = query
    query_t_ref[...] = query.T


def source_side(t, src, dst, own, rel):
    dim, slots = rel.shape
    rows = 2 * own[0].shape[1]
    sds = lambda *shape: jax.ShapeDtypeStruct(shape, BF)
    return pl.pallas_call(
        functools.partial(source_kernel, t),
        in_specs=[vmem()] * 5,
        out_specs=[vmem()] * 6,
        out_shape=[
            sds(dim, slots), sds(slots, dim), sds(dim, slots),
            sds(rows, slots), sds(rows, slots), sds(slots, rows),
        ],
        compiler_params=params(),
        cost_estimate=cost(dim * slots, dim * slots),
        name="source_side",
    )(src, dst, *own, rel)


def target_kernel(
    t, shape, cnt_ref, neg_ref, far0, far1, query_ref, query_t_ref, d_hot_ref, d_hot_t_ref,
    gd_mine, gd_other, o_ref, w_ref, gpos_ref, cnt, neg, sems, d_scr,
):
    limits = Limits(t, cnt_ref, neg_ref, cnt, neg, sems)
    half = far0.shape[1]
    far = jnp.concatenate([far0[...], far1[...]], axis=1)
    target = mm(far, d_hot_ref[...])
    gpos_ref[...] = target_side(
        shape, limits, query_ref[...], query_t_ref, target, o_ref, d_scr, w_ref
    )
    gd = mm(d_scr[...].astype(BF), d_hot_t_ref[...])
    gd_mine[...] = gd[:, :half]
    gd_other[...] = gd[:, half:].astype(BF)


def target_grad(t, shape, cnt, neg, far, query, query_t, d_hot, d_hot_t):
    dim, slots = query.shape
    half = far[0].shape[1]
    width = shape[2]
    sds = jax.ShapeDtypeStruct
    return pl.pallas_call(
        functools.partial(target_kernel, t, shape),
        in_specs=[anywhere()] * 2 + [vmem()] * 6,
        out_specs=[vmem()] * 5,
        out_shape=[
            sds((dim, half), F32),
            sds((dim, half), BF),
            sds((dim, slots), BF),
            sds((width, slots), BF),
            sds((1, slots), F32),
        ],
        scratch_shapes=Limits.scratch(shape) + [pltpu.VMEM((dim, slots), F32)],
        compiler_params=params(),
        cost_estimate=cost(4 * dim * slots * (2 * half + width), 12 * dim * slots),
        name="target_grad",
    )(cnt, neg, *far, query, query_t, d_hot, d_hot_t)


def source_grad_kernel(
    t, shape, cnt_ref, neg_ref, _, o_ref, w_ref, gpos_ref, source_ref, rel_ref, s_hot_ref,
    gs_mine, gs_other, drel_ref, cnt, neg, sems,
):
    limits = Limits(t, cnt_ref, neg_ref, cnt, neg, sems)
    limits.wait()
    half = gs_mine.shape[1]
    dq = make_dquery(shape, limits, gpos_ref[...], o_ref, w_ref)
    drel_ref[...] = conj_times(dq, source_ref[...].astype(F32))
    gs = mm(conj_times(dq, rel_ref[...].astype(F32)), s_hot_ref[...], NT)
    gs_mine[...] = gs[:, :half]
    gs_other[...] = gs[:, half:].astype(BF)


def source_grad(t, shape, cnt, neg, after, target, weight, gpos, source, rel, s_hot):
    dim, slots = rel.shape
    half = s_hot.shape[0] // 2
    sds = jax.ShapeDtypeStruct
    return pl.pallas_call(
        functools.partial(source_grad_kernel, t, shape),
        in_specs=[anywhere()] * 3 + [vmem()] * 6,
        out_specs=[vmem()] * 3,
        out_shape=[sds((dim, half), F32), sds((dim, half), BF), sds((dim, slots), BF)],
        scratch_shapes=Limits.scratch(shape),
        compiler_params=params(),
        cost_estimate=cost(dim * slots, dim * slots),
        name="source_grad",
    )(cnt, neg, after, target, weight, gpos, source, rel, s_hot)


def last_kernel(
    t, shape, cnt_ref, neg_ref, far0, far1, query_ref, query_t_ref, d_hot_ref, source_ref, rel_ref,
    drel_ref, dsource_ref, dterm_ref, cnt, neg, sems, o_scr, d_scr, w_scr,
):
    limits = Limits(t, cnt_ref, neg_ref, cnt, neg, sems)
    far = jnp.concatenate([far0[...], far1[...]], axis=1)
    target = mm(far, d_hot_ref[...])
    gpos = target_side(
        shape, limits, query_ref[...], query_t_ref, target, o_scr, d_scr, w_scr
    )
    dterm_ref[...] = d_scr[...].astype(BF)
    dq = make_dquery(shape, limits, gpos, o_scr, w_scr)
    drel_ref[...] = conj_times(dq, source_ref[...].astype(F32))
    dsource_ref[...] = conj_times(dq, rel_ref[...].astype(F32))


def last_terms(t, shape, cnt, neg, far, query, query_t, d_hot, source, rel):
    dim, slots = query.shape
    return pl.pallas_call(
        functools.partial(last_kernel, t, shape),
        in_specs=[anywhere()] * 2 + [vmem()] * 7,
        out_specs=[vmem()] * 3,
        out_shape=[jax.ShapeDtypeStruct((dim, slots), BF)] * 3,
        scratch_shapes=Limits.scratch(shape)
        + [
            pltpu.VMEM((dim, slots), BF),
            pltpu.VMEM((dim, slots), F32),
            pltpu.VMEM((shape[2], slots), BF),
        ],
        compiler_params=params(),
        cost_estimate=cost(6 * dim * slots * shape[2], 12 * dim * slots),
        name="last_terms",
    )(cnt, neg, *far, query, query_t, d_hot, source, rel)


def both_kernel(dsource_ref, s_hot_ref, dterm_ref, d_hot_t_ref, gs_mine, gs_other, gd_mine, gd_other):
    half = gs_mine.shape[1]
    for terms, hot, dims, mine, other in (
        (dterm_ref, d_hot_t_ref, NN, gd_mine, gd_other),
        (dsource_ref, s_hot_ref, NT, gs_mine, gs_other),
    ):
        grad = mm(terms[...], hot[...], dims)
        mine[...] = grad[:, :half]
        other[...] = grad[:, half:].astype(BF)


def both_grads(dsource, s_hot, dterm, d_hot_t):
    dim, slots = dterm.shape
    half = s_hot.shape[0] // 2
    sds = jax.ShapeDtypeStruct
    return pl.pallas_call(
        both_kernel,
        in_specs=[vmem()] * 4,
        out_specs=[vmem()] * 4,
        out_shape=[sds((dim, half), F32), sds((dim, half), BF)] * 2,
        compiler_params=params(),
        cost_estimate=cost(8 * dim * slots * half, 12 * dim * slots),
        name="both_grads",
    )(dsource, s_hot, dterm, d_hot_t)


def update_kernel(n_grads, last, *refs):
    ent_ref, state_ref, grads = refs[0], refs[1], refs[2 : 2 + n_grads]
    grad = grads[0][...].astype(F32)
    for g in grads[1:]:
        grad = grad + g[...].astype(F32)
    dim = grad.shape[0]
    state = state_ref[...] + jnp.sum(grad * grad, axis=0, keepdims=True) / dim
    new = ent_ref[...] - grad * (learn_rate / jnp.sqrt(state))
    if last:
        refs[-1][:dim] = new
        refs[-1][dim:] = jnp.broadcast_to(state, (refs[-1].shape[0] - dim, state.shape[1]))
    else:
        refs[-3][...] = new
        refs[-2][...] = state
        refs[-1][...] = new.astype(BF)


def update(ent, state, grads, after, last=False):
    dim, half = ent.shape
    sds = jax.ShapeDtypeStruct
    outs = [sds((dim, half), F32), sds((1, half), F32), sds((dim, half), BF)]
    if last:
        outs = [sds((dim + 8, half), F32)]
    return pl.pallas_call(
        functools.partial(update_kernel, len(grads), last),
        in_specs=[vmem()] * (2 + len(grads)) + [anywhere()] * len(after),
        out_specs=[vmem()] * len(outs),
        out_shape=outs,
        compiler_params=params(),
        cost_estimate=cost(10 * dim * half, 16 * dim * half),
        name="update",
    )(ent, state, *grads, *after)


def pair_kernel(a_ref, b_ref, out_ref):
    out_ref[...] = (a_ref[...] + b_ref[...].astype(F32)).astype(out_ref.dtype)


def sum_pair(a, b, dtype=BF):
    return pl.pallas_call(
        pair_kernel,
        in_specs=[vmem()] * 2,
        out_specs=vmem(),
        out_shape=jax.ShapeDtypeStruct(a.shape, dtype),
        compiler_params=params(),
        name="sum_pair",
    )(a, b)


def held_kernel(x_ref, *refs):
    pass


def held(x, after):
    return pl.pallas_call(
        held_kernel,
        in_specs=[anywhere()] * (1 + len(after)),
        out_specs=anywhere(),
        out_shape=jax.ShapeDtypeStruct(x.shape, x.dtype),
        input_output_aliases={0: 0},
        compiler_params=params(),
        name="held",
    )(x, *after)


def whole_kernel(mine, theirs, ent_out, state_out, token):
    token[...] = jnp.zeros_like(token)
    dim, rows = ent_out.shape
    half = rows // 2
    edge = place()[2]
    for core, part in ((edge, mine), (1 - edge, theirs)):
        at = pl.ds(pl.multiple_of(core * half, half), half)
        ent_out[:, at] = part[:dim]
        state_out[:, at] = part[dim : dim + 1]


def whole_partition(mine, theirs):
    dim, half = mine.shape[0] - 8, mine.shape[1]
    return pl.pallas_call(
        whole_kernel,
        in_specs=[vmem()] * 2,
        out_specs=[vmem()] * 3,
        out_shape=[
            jax.ShapeDtypeStruct((dim, 2 * half), F32),
            jax.ShapeDtypeStruct((1, 2 * half), F32),
            jax.ShapeDtypeStruct((8, 128), F32),
        ],
        compiler_params=params(),
        name="whole_partition",
    )(mine, theirs)


def first_column(owner, core, w):
    return pl.multiple_of((2 * owner + core) * w, w)


def pieces_kernel(t, nz, same, ids_ref, drel_ref, acc_ref, *refs):
    mine, other = refs[-nz - 1 : -1], refs[-1]
    w = other.shape[2]
    z, x, edge = place()
    drel = drel_ref[...]
    for k in range(nz):
        owner = 2 * lax.rem(z + k, nz) + (x if same else 1 - x)
        at = [first_column(owner, core, w) for core in (edge, 1 - edge)]
        hot = jnp.concatenate([one_hot(ids_ref, t, w, lambda i, lo=lo: i - lo) for lo in at], axis=0)
        part = mm(drel, hot, NT)
        mine[k][...] = acc_ref[:, pl.ds(at[0], w)] + part[:, :w]
        other[k] = (acc_ref[:, pl.ds(at[1], w)] + part[:, w:]).astype(BF)


def pieces(t, n, same, rel_ids, drel, acc, after):
    dim, rels = acc.shape
    w = rels // (2 * n)
    sds = jax.ShapeDtypeStruct
    out = pl.pallas_call(
        functools.partial(pieces_kernel, t, n // 2, same),
        in_specs=[vmem()] * 3 + [anywhere()] * len(after),
        out_specs=[vmem()] * (n // 2 + 1),
        out_shape=[sds((dim, w), F32)] * (n // 2) + [sds((n // 2, dim, w), BF)],
        compiler_params=params(),
        cost_estimate=cost(dim * rels * drel.shape[1], 4 * dim * rels),
        name="pieces",
    )(rel_ids, drel, acc, *after)
    return out[:-1], out[-1]


def add_kernel(n, *refs):
    for k in range(n):
        refs[n + 1 + k][...] = (refs[k][...] + refs[n][k].astype(F32)).astype(BF)


def add_each(mine, theirs):
    n = len(mine)
    return pl.pallas_call(
        functools.partial(add_kernel, n),
        in_specs=[vmem()] * (n + 1),
        out_specs=[vmem()] * n,
        out_shape=[jax.ShapeDtypeStruct(x.shape, BF) for x in mine],
        compiler_params=params(),
        name="add_each",
    )(*mine, theirs)


def sum_kernel(k, count, mine, theirs, *refs):
    total = mine[...] + theirs[k].astype(F32)
    for r in refs[:count]:
        total = total + r[...].astype(F32)
    refs[-1][...] = total.astype(BF)


def sum_piece(k, mine, theirs, parts, after):
    return pl.pallas_call(
        functools.partial(sum_kernel, k, len(parts)),
        in_specs=[vmem()] * (2 + len(parts)) + [anywhere()] * len(after),
        out_specs=vmem(),
        out_shape=jax.ShapeDtypeStruct(mine.shape, BF),
        compiler_params=params(),
        name="sum_piece",
    )(mine, theirs, *parts, *after)


def relnew_kernel(nz, same, ks, rel_ref, state_ref, *refs):
    got = refs[: 2 * len(ks)]
    rel_out, state_out, buf, sems = refs[-4:]
    w = got[0].shape[1]
    state_out[...] = refs[len(got) + (0 if same else 1)][...]
    z, x, edge = place()
    copies = []
    for i, grad_ref in enumerate(got):
        owner = 2 * lax.rem(z + nz - ks[i // 2], nz) + (x if same else 1 - x)
        at = pl.ds(first_column(owner, edge if i % 2 == 0 else 1 - edge, w), w)
        grad = grad_ref[...].astype(F32)
        state = state_ref[:, at] + jnp.sum(grad * grad, axis=0, keepdims=True) / grad.shape[0]
        state_out[:, at] = state
        buf[i] = rel_ref[:, at] - grad * (learn_rate / jnp.sqrt(state))
        copy = pltpu.make_async_copy(buf.at[i], rel_out.at[:, at], sems.at[i])
        copy.start()
        copies.append(copy)
    for copy in copies:
        copy.wait()


def relnew(nz, same, ks, relations, state, got, before, after):
    dim, rels = relations.shape
    w = got[0].shape[1]
    start = [state] if before is None else list(before)
    return pl.pallas_call(
        functools.partial(relnew_kernel, nz, same, ks),
        in_specs=[vmem()] * (2 + len(got)) + ([anywhere()] if before else [])
        + [vmem()]
        + [anywhere()] * len(after),
        out_specs=[anywhere(), vmem()],
        out_shape=[jax.ShapeDtypeStruct((dim, rels), F32), jax.ShapeDtypeStruct((1, rels), F32)],
        input_output_aliases={2 + len(got): 0} if before else {},
        scratch_shapes=[pltpu.VMEM((len(got), dim, w), F32), pltpu.SemaphoreType.DMA((len(got),))],
        compiler_params=params(),
        cost_estimate=cost(4 * dim * w * len(got), 4 * dim * w * len(got)),
        name="relnew",
    )(relations, state, *got, *start, *after)


def relation_update(t, rel_ids, drel, acc, relations, state, gd_other, gd, grads, finish):
    n = lax.axis_size("dom")
    dim, rels = relations.shape
    if n % 2 or rels % (256 * n):
        total = lax.psum(relsum(t, rel_ids, drel, acc, rels), ("dom", "edge"))
        state = state + jnp.mean(total * total, axis=0)
        return relations - learn_rate * total / jnp.sqrt(state)[None, :], state, finish([])
    nz = n // 2
    near = sorted(range(nz), key=lambda k: min(k, nz - k))
    mine_x, other_x = pieces(t, n, False, rel_ids, drel, acc, [gd_other])
    mine_s, other_s = pieces(t, n, True, rel_ids, drel, acc, [gd])
    to_x = add_each(mine_x, across(other_x))
    theirs = across(other_s)
    from_x = {k: beside(to_x[k]) for k in reversed(near)}
    from_z = []
    for i, k in enumerate(reversed(near[1:])):
        after = [grads[i]] if i < len(grads) else []
        piece = sum_piece(k, mine_s[k], theirs, [from_x[k]], after)
        from_z.append(shifted(piece, 2 * k))
    done = finish([piece])
    summed = sum_piece(0, mine_s[0], theirs, [from_x[0]] + from_z, [])
    got = [summed if k == 0 else shifted(summed, 2 * k) for k in range(nz)]
    got_x = [beside(piece) for piece in got]
    state = state.reshape(1, rels)
    pairs = lambda ks, parts: [y for k in ks for y in (parts[k], across(parts[k]))]
    early, late = near[:-1], near[-1:]
    new = relnew(nz, True, near, relations, state, pairs(near, got), None, [done[2]])
    new = relnew(nz, False, early, relations, state, pairs(early, got_x), new, [])
    rel_new, state_new = relnew(nz, False, late, relations, state, pairs(late, got_x), new, [])
    return rel_new, state_new.reshape(rels), done


def on_device(
    entities,
    entity_state,
    relations,
    relation_state,
    src_rows,
    rel_ids,
    dst_rows,
    counts,
    neg_blocks,
):
    rounds = src_rows.shape[0]
    rels = relations.shape[1]
    shape = src_rows.shape
    cnt, neg = counts.T, neg_blocks.T
    g_mine, g_other, drel, rel16, ent, state = first_round(
        cnt, neg, src_rows, dst_rows, rel_ids, entities, entity_state.reshape(1, -1), relations
    )
    acc = relsum(0, rel_ids, drel, None, rels)
    ent, state, low = update(ent, state, [g_mine, across(g_other)], [])
    rel = relvec(1, rel_ids, rel16)
    for t in range(1, rounds):
        far = shifted(low, -t)
        own = (low, across(low))
        query, query_t, source, s_hot, d_hot, d_hot_t = source_side(t, src_rows, dst_rows, own, rel)
        far = held(far, [query, acc])
        far = (far, across(far))
        if t == rounds - 1:
            break
        gd_mine, gd_other, target, weight, gpos = target_grad(
            t, shape, cnt, neg, far, query, query_t, d_hot, d_hot_t
        )
        gd = sum_pair(gd_mine, across(gd_other))
        gs_mine, gs_other, drel = source_grad(
            t, shape, cnt, neg, gd, target, weight, gpos, source, rel, s_hot
        )
        acc = relsum(t, rel_ids, drel, acc, rels)
        rel = relvec(t + 1, rel_ids, rel16)
        grads = [sum_pair(gs_mine, shifted(gd, t), F32), across(gs_other)]
        ent, state, low = update(ent, state, grads, [rel])
    drel, dsource, dterm = last_terms(t, shape, cnt, neg, far, query, query_t, d_hot, source, rel)
    gs_mine, gs_other, gd_mine, gd_other = both_grads(dsource, s_hot, dterm, d_hot_t)
    gd = sum_pair(gd_mine, across(gd_other))

    grads = [across(gs_other), shifted(gd, t)]

    def finish(after):
        (mine,) = update(ent, state, [gs_mine, *grads], after, last=True)
        return whole_partition(mine, across(mine))

    rel_new, rel_state, done = relation_update(
        t, rel_ids, drel, acc, relations, relation_state, gd_other, gd, grads, finish
    )
    return (done[0], done[1].reshape(-1), rel_new, rel_state)


def solution(mesh):
    return jax.shard_map(
        on_device,
        mesh=mesh,
        in_specs=(
            P(None, ("groups", "dom")),
            P(("groups", "dom")),
            P(None, "groups"),
            P("groups"),
            P(None, ("groups", "dom", "edge"), None),
            P(None, ("groups", "dom", "edge"), None),
            P(None, ("groups", "dom", "edge"), None),
            P(None, ("groups", "dom", "edge")),
            P(None, ("groups", "dom", "edge")),
        ),
        out_specs=(
            P(None, ("groups", "dom")),
            P(("groups", "dom")),
            P(None, "groups"),
            P("groups"),
        ),
        check_vma=False,
    )
```

profile of v0, /device:TPU:0, one launch (start us, length us, event | category | flops | bytes accessed | tf_op | source)
XLA Modules:
  0.0 142.6 jit_solution(14005525515725800001)
XLA Ops:
  0.6 5.3 %first_round.1 = (f32[400,128]{1,0:T(8,128)S(1)}, bf16[400,128]{1,0:T(8,128)(2,1)S(1)}, bf16[400,512]{1,0:T(8,128)(2,1)S(1)}, bf16[400,2048]{1,0:T(8,128)(2,1)S(...) custom-call(s32[4,6]{1,0:T(4,128)} %bitcast.6, s32[4,6]{1,0:T(4,128)} %bitcast.16, s32[6,4,128]{2,1,0:T(4,128)} %src_ref.11, ...), custom_call_target="tpu_custom_call" | custom-call | flops 1258291200 | bytes 6553600 | tf_op jit(solution)/shard_map/first_round/pallas_call | solution.py:299
  6.5 0.9 collective-permute-done.refs_3_
  7.9 5.7 %collective-permute-start.1 = (bf16[400,128]{1,0:T(8,128)(2,1)S(1)}, bf16[400,128]{1,0:T(8,128)(2,1)S(1)}, u32[]{:S(2)}, u32[]{:S(2)}) collective-permute-start(bf16[400,128]{1,0:T(8,128)(2,1)S(1)} %get-tuple-element.123.own0), channel_id=1, source_target_pairs={{0,14},{2,0},{4,2},{6,4},{8,6},{10,8},{12,10},{14,12},{1,15},{3,1}... | collective-permute-start | bytes 307208 | tf_op jit(solution)/shard_map/ppermute | solution.py:49
  13.6 1.0 relvec.5.rel_ref
  14.7 1.9 %relsum.5.refs_1_.refs_0_ = f32[400,2048]{1,0:T(8,128)S(1)} custom-call(s32[6,4,128]{2,1,0:T(4,128)S(1)} %copy-done.1, bf16[400,512]{1,0:T(8,128)(2,1)S(1)} %get-tuple-element.126.drel_ref), custom_call_target="tpu_custom_call" | custom-call | flops 204800 | bytes 204800 | tf_op jit(solution)/shard_map/relsum/pallas_call | solution.py:113
  16.6 0.6 source_side.5
  17.4 1.2 collective-permute-done.3.far1
  18.6 1.6 %target_grad.4 = (f32[400,128]{1,0:T(8,128)S(1)}, bf16[400,128]{1,0:T(8,128)(2,1)S(1)}, bf16[400,512]{1,0:T(8,128)(2,1)S(1)}, bf16[128,512]{1,0:T(8,128)(2,1)S(1)}, f32[1,512]{1,0:T(1,128)S(1)}) custom-call(s32[4,6]{1,0:T(4,128)S(1)} %bitcast.7, s32[4,6]{1,0:T(4,128)S(1)} %bitcast.17, bf16[400,128]{1,0:T(8,128)(2,1)S(1)} %held.5.far0, ...), custom_call_target="tpu_custom_call" | custom-call | flops 314572800 | bytes 2457600 | tf_op jit(solution)/shard_map/target_grad/pallas_call | solution.py:388
  20.4 1.2 collective-permute-done.4.b_ref
  21.7 1.5 %source_grad.4 = (f32[400,128]{1,0:T(8,128)S(1)}, bf16[400,128]{1,0:T(8,128)(2,1)S(1)}, bf16[400,512]{1,0:T(8,128)(2,1)S(1)}) custom-call(s32[4,6]{1,0:T(4,128)S(1)} %bitcast.8, s32[4,6]{1,0:T(4,128)S(1)} %bitcast.18, bf16[400,128]{1,0:T(8,128)(2,1)S(1)} %sum_pair.9._, bf16[400,512]{1,0:T(8,128)(2,1)S(1)} %get-tuple-element.132.o_ref, ...), custom_call_target="tpu_custom_call" | custom-call | flops 204800 | bytes 204800 | tf_op jit(solution)/shard_map/source_grad/pallas_call | solution.py:424
  23.4 1.0 relvec.6.refs_4_.rel_ref
  24.4 4.9 %collective-permute-done.5.b_ref = bf16[400,128]{1,0:T(8,128)(2,1)S(1)} collective-permute-done((bf16[400,128]{1,0:T(8,128)(2,1)S(1)}, bf16[400,128]{1,0:T(8,128)(2,1)S(1)}, u32[]{:S(2)}, u32[]{:S(2)}) %collective-permute-start.5) | collective-permute-done | bytes 102432 | tf_op jit(solution)/shard_map/ppermute | solution.py:49
  29.7 2.2 %relsum.6.refs_1_.refs_0_ = f32[400,2048]{1,0:T(8,128)S(1)} custom-call(s32[6,4,128]{2,1,0:T(4,128)S(1)} %copy-done.1, bf16[400,512]{1,0:T(8,128)(2,1)S(1)} %get-tuple-element.143.drel_ref, f32[400,2048]{1,0:T(8,128)S(1)} %relsum.5.refs_1_.refs_0_), custom_call_target="tpu_custom_call", output_to_operand_aliasing={{}: (2, {})} | custom-call | flops 204800 | bytes 204800 | tf_op jit(solution)/shard_map/relsum/pallas_call | solution.py:113
  32.5 2.4 %collective-permute-done.7.x_ref = bf16[400,128]{1,0:T(8,128)(2,1)S(1)} collective-permute-done((bf16[400,128]{1,0:T(8,128)(2,1)S(1)}, bf16[400,128]{1,0:T(8,128)(2,1)S(1)}, u32[]{:S(2)}, u32[]{:S(2)}) %collective-permute-start.7) | collective-permute-done | bytes 102432 | tf_op jit(solution)/shard_map/ppermute | solution.py:49
  34.8 1.3 collective-permute-done.9.far1
  36.1 1.6 %target_grad.5 = (f32[400,128]{1,0:T(8,128)S(1)}, bf16[400,128]{1,0:T(8,128)(2,1)S(1)}, bf16[400,512]{1,0:T(8,128)(2,1)S(1)}, bf16[128,512]{1,0:T(8,128)(2,1)S(1)}, f32[1,512]{1,0:T(1,128)S(1)}) custom-call(s32[4,6]{1,0:T(4,128)S(1)} %bitcast.9, s32[4,6]{1,0:T(4,128)S(1)} %bitcast.19, bf16[400,128]{1,0:T(8,128)(2,1)S(1)} %held.6.far0, ...), custom_call_target="tpu_custom_call" | custom-call | flops 314572800 | bytes 2457600 | tf_op jit(solution)/shard_map/target_grad/pallas_call | solution.py:388
  37.9 1.2 collective-permute-done.10.b_ref
  39.3 1.5 %source_grad.5 = (f32[400,128]{1,0:T(8,128)S(1)}, bf16[400,128]{1,0:T(8,128)(2,1)S(1)}, bf16[400,512]{1,0:T(8,128)(2,1)S(1)}) custom-call(s32[4,6]{1,0:T(4,128)S(1)} %bitcast.10, s32[4,6]{1,0:T(4,128)S(1)} %bitcast.20, bf16[400,128]{1,0:T(8,128)(2,1)S(1)} %sum_pair.11._, bf16[400,512]{1,0:T(8,128)(2,1)S(1)} %get-tuple-element.149.o_ref, ...), custom_call_target="tpu_custom_call" | custom-call | flops 204800 | bytes 204800 | tf_op jit(solution)/shard_map/source_grad/pallas_call | solution.py:424
  41.0 1.0 relvec.7.refs_4_.rel_ref
  42.1 4.0 %collective-permute-done.11.b_ref = bf16[400,128]{1,0:T(8,128)(2,1)S(1)} collective-permute-done((bf16[400,128]{1,0:T(8,128)(2,1)S(1)}, bf16[400,128]{1,0:T(8,128)(2,1)S(1)}, u32[]{:S(2)}, u32[]{:S(2)}) %collective-permute-start.11) | collective-permute-done | bytes 102432 | tf_op jit(solution)/shard_map/ppermute | solution.py:49
  46.4 2.2 %relsum.7.refs_1_.refs_0_ = f32[400,2048]{1,0:T(8,128)S(1)} custom-call(s32[6,4,128]{2,1,0:T(4,128)S(1)} %copy-done.1, bf16[400,512]{1,0:T(8,128)(2,1)S(1)} %get-tuple-element.160.drel_ref, f32[400,2048]{1,0:T(8,128)S(1)} %relsum.6.refs_1_.refs_0_), custom_call_target="tpu_custom_call", output_to_operand_aliasing={{}: (2, {})} | custom-call | flops 204800 | bytes 204800 | tf_op jit(solution)/shard_map/relsum/pallas_call | solution.py:113
  49.2 3.3 %collective-permute-done.13.x_ref = bf16[400,128]{1,0:T(8,128)(2,1)S(1)} collective-permute-done((bf16[400,128]{1,0:T(8,128)(2,1)S(1)}, bf16[400,128]{1,0:T(8,128)(2,1)S(1)}, u32[]{:S(2)}, u32[]{:S(2)}) %collective-permute-start.13) | collective-permute-done | bytes 102432 | tf_op jit(solution)/shard_map/ppermute | solution.py:49
  52.5 1.3 collective-permute-done.15.far1
  53.8 1.6 %target_grad.6 = (f32[400,128]{1,0:T(8,128)S(1)}, bf16[400,128]{1,0:T(8,128)(2,1)S(1)}, bf16[400,512]{1,0:T(8,128)(2,1)S(1)}, bf16[128,512]{1,0:T(8,128)(2,1)S(1)}, f32[1,512]{1,0:T(1,128)S(1)}) custom-call(s32[4,6]{1,0:T(4,128)S(1)} %bitcast.11, s32[4,6]{1,0:T(4,128)S(1)} %bitcast.21, bf16[400,128]{1,0:T(8,128)(2,1)S(1)} %held.7.far0, ...), custom_call_target="tpu_custom_call" | custom-call | flops 314572800 | bytes 2457600 | tf_op jit(solution)/shard_map/target_grad/pallas_call | solution.py:388
  55.6 1.2 collective-permute-done.16.b_ref
  56.8 1.5 %source_grad.6 = (f32[400,128]{1,0:T(8,128)S(1)}, bf16[400,128]{1,0:T(8,128)(2,1)S(1)}, bf16[400,512]{1,0:T(8,128)(2,1)S(1)}) custom-call(s32[4,6]{1,0:T(4,128)S(1)} %bitcast.12, s32[4,6]{1,0:T(4,128)S(1)} %bitcast.22, bf16[400,128]{1,0:T(8,128)(2,1)S(1)} %sum_pair.13._, bf16[400,512]{1,0:T(8,128)(2,1)S(1)} %get-tuple-element.166.o_ref, ...), custom_call_target="tpu_custom_call" | custom-call | flops 204800 | bytes 204800 | tf_op jit(solution)/shard_map/source_grad/pallas_call | solution.py:424
  58.5 1.0 relvec.8.refs_4_.rel_ref
  59.6 6.2 %collective-permute-done.17.b_ref = bf16[400,128]{1,0:T(8,128)(2,1)S(1)} collective-permute-done((bf16[400,128]{1,0:T(8,128)(2,1)S(1)}, bf16[400,128]{1,0:T(8,128)(2,1)S(1)}, u32[]{:S(2)}, u32[]{:S(2)}) %collective-permute-start.17) | collective-permute-done | bytes 102432 | tf_op jit(solution)/shard_map/ppermute | solution.py:49
  66.1 2.2 %relsum.8.refs_1_.refs_0_ = f32[400,2048]{1,0:T(8,128)S(1)} custom-call(s32[6,4,128]{2,1,0:T(4,128)S(1)} %copy-done.1, bf16[400,512]{1,0:T(8,128)(2,1)S(1)} %get-tuple-element.177.drel_ref, f32[400,2048]{1,0:T(8,128)S(1)} %relsum.7.refs_1_.refs_0_), custom_call_target="tpu_custom_call", output_to_operand_aliasing={{}: (2, {})} | custom-call | flops 204800 | bytes 204800 | tf_op jit(solution)/shard_map/relsum/pallas_call | solution.py:113
  68.9 4.1 %collective-permute-done.19.x_ref = bf16[400,128]{1,0:T(8,128)(2,1)S(1)} collective-permute-done((bf16[400,128]{1,0:T(8,128)(2,1)S(1)}, bf16[400,128]{1,0:T(8,128)(2,1)S(1)}, u32[]{:S(2)}, u32[]{:S(2)}) %collective-permute-start.19) | collective-permute-done | bytes 102432 | tf_op jit(solution)/shard_map/ppermute | solution.py:49
  73.1 1.2 collective-permute-done.21.far1
  74.3 1.6 %target_grad.7 = (f32[400,128]{1,0:T(8,128)S(1)}, bf16[400,128]{1,0:T(8,128)(2,1)S(1)}, bf16[400,512]{1,0:T(8,128)(2,1)S(1)}, bf16[128,512]{1,0:T(8,128)(2,1)S(1)}, f32[1,512]{1,0:T(1,128)S(1)}) custom-call(s32[4,6]{1,0:T(4,128)S(1)} %bitcast.13, s32[4,6]{1,0:T(4,128)S(1)} %bitcast.23, bf16[400,128]{1,0:T(8,128)(2,1)S(1)} %held.8.far0, ...), custom_call_target="tpu_custom_call" | custom-call | flops 314572800 | bytes 2457600 | tf_op jit(solution)/shard_map/target_grad/pallas_call | solution.py:388
  76.1 1.1 collective-permute-done.22.b_ref
  77.4 1.5 %source_grad.7 = (f32[400,128]{1,0:T(8,128)S(1)}, bf16[400,128]{1,0:T(8,128)(2,1)S(1)}, bf16[400,512]{1,0:T(8,128)(2,1)S(1)}) custom-call(s32[4,6]{1,0:T(4,128)S(1)} %bitcast.14, s32[4,6]{1,0:T(4,128)S(1)} %bitcast.24, bf16[400,128]{1,0:T(8,128)(2,1)S(1)} %sum_pair.15._, bf16[400,512]{1,0:T(8,128)(2,1)S(1)} %get-tuple-element.183.o_ref, ...), custom_call_target="tpu_custom_call" | custom-call | flops 204800 | bytes 204800 | tf_op jit(solution)/shard_map/source_grad/pallas_call | solution.py:424
  79.1 1.0 relvec.9.refs_4_.rel_ref
  80.1 5.0 %collective-permute-done.23.b_ref = bf16[400,128]{1,0:T(8,128)(2,1)S(1)} collective-permute-done((bf16[400,128]{1,0:T(8,128)(2,1)S(1)}, bf16[400,128]{1,0:T(8,128)(2,1)S(1)}, u32[]{:S(2)}, u32[]{:S(2)}) %collective-permute-start.23) | collective-permute-done | bytes 102432 | tf_op jit(solution)/shard_map/ppermute | solution.py:49
  85.7 2.2 %relsum.9.refs_1_.acc_ref = f32[400,2048]{1,0:T(8,128)S(1)} custom-call(s32[6,4,128]{2,1,0:T(4,128)S(1)} %copy-done.1, bf16[400,512]{1,0:T(8,128)(2,1)S(1)} %get-tuple-element.194.drel_ref, f32[400,2048]{1,0:T(8,128)S(1)} %relsum.8.refs_1_.refs_0_), custom_call_target="tpu_custom_call", output_to_operand_aliasing={{}: (2, {})} | custom-call | flops 204800 | bytes 204800 | tf_op jit(solution)/shard_map/relsum/pallas_call | solution.py:113
  87.9 0.6 source_side.9
  88.5 4.3 %collective-permute-done.25.x_ref = bf16[400,128]{1,0:T(8,128)(2,1)S(1)} collective-permute-done((bf16[400,128]{1,0:T(8,128)(2,1)S(1)}, bf16[400,128]{1,0:T(8,128)(2,1)S(1)}, u32[]{:S(2)}, u32[]{:S(2)}) %collective-permute-start.25) | collective-permute-done | bytes 102432 | tf_op jit(solution)/shard_map/ppermute | solution.py:49
  92.8 1.3 collective-permute-done.27.far1
  94.1 1.7 %last_terms.1 = (bf16[400,512]{1,0:T(8,128)(2,1)S(1)}, bf16[400,512]{1,0:T(8,128)(2,1)S(1)}, bf16[400,512]{1,0:T(8,128)(2,1)S(1)}) custom-call(s32[4,6]{1,0:T(4,128)S(1)} %bitcast.15, s32[4,6]{1,0:T(4,128)S(1)} %bitcast.25, bf16[400,128]{1,0:T(8,128)(2,1)S(1)} %held.9.far0, bf16[400,128]{1,0:T(8,128)(2,1)S(1)} %collective-permute-done.27.far1, ...), custom_call_target="tpu_custom_call" | custom-call | flops 157286400 | bytes 2457600 | tf_op jit(solution)/shard_map/last_terms/pallas_call | solution.py:454
  96.4 0.7 pieces.3
  97.6 0.7 pieces.2
  99.0 0.9 collective-permute-start.33
  99.9 1.2 collective-permute-start.36
  101.1 3.8 %collective-permute-start.38 = (bf16[400,128]{1,0:T(8,128)(2,1)S(1)}, bf16[400,128]{1,0:T(8,128)(2,1)S(1)}, u32[]{:S(2)}, u32[]{:S(2)}) collective-permute-start(bf16[400,128]{1,0:T(8,128)(2,1)S(1)} %get-tuple-element.222), channel_id=1, source_target_pairs={{0,2},{2,0},{4,6},{6,4},{8,10},{10,8},{12,14},{14,12},{1,3},{3,1},... | collective-permute-start | bytes 307208 | tf_op jit(solution)/shard_map/ppermute | solution.py:54
  106.0 3.1 %collective-permute-done.36.refs_0_ = bf16[400,128]{1,0:T(8,128)(2,1)S(1)} collective-permute-done((bf16[400,128]{1,0:T(8,128)(2,1)S(1)}, bf16[400,128]{1,0:T(8,128)(2,1)S(1)}, u32[]{:S(2)}, u32[]{:S(2)}) %collective-permute-start.36) | collective-permute-done | bytes 102432 | tf_op jit(solution)/shard_map/ppermute | solution.py:54
  109.3 2.1 %collective-permute-done.38.refs_0_ = bf16[400,128]{1,0:T(8,128)(2,1)S(1)} collective-permute-done((bf16[400,128]{1,0:T(8,128)(2,1)S(1)}, bf16[400,128]{1,0:T(8,128)(2,1)S(1)}, u32[]{:S(2)}, u32[]{:S(2)}) %collective-permute-start.38) | collective-permute-done | bytes 102432 | tf_op jit(solution)/shard_map/ppermute | solution.py:54
  111.4 2.4 %collective-permute-start.39 = (bf16[400,128]{1,0:T(8,128)(2,1)S(1)}, bf16[400,128]{1,0:T(8,128)(2,1)S(1)}, u32[]{:S(2)}, u32[]{:S(2)}) collective-permute-start(bf16[400,128]{1,0:T(8,128)(2,1)S(1)} %sum_piece.6), channel_id=1, source_target_pairs={{0,12},{2,14},{4,0},{6,2},{8,4},{10,6},{12,8},{14,10},{1,13},{3,15... | collective-permute-start | bytes 307208 | tf_op jit(solution)/shard_map/ppermute | solution.py:49
  114.0 2.3 %collective-permute-done.37.refs_1_ = bf16[400,128]{1,0:T(8,128)(2,1)S(1)} collective-permute-done((bf16[400,128]{1,0:T(8,128)(2,1)S(1)}, bf16[400,128]{1,0:T(8,128)(2,1)S(1)}, u32[]{:S(2)}, u32[]{:S(2)}) %collective-permute-start.37) | collective-permute-done | bytes 102432 | tf_op jit(solution)/shard_map/ppermute | solution.py:49
  116.3 0.7 collective-permute-done.39.refs_2_
  117.1 3.4 %collective-permute-start.49 = (bf16[400,128]{1,0:T(8,128)(2,1)S(1)}, bf16[400,128]{1,0:T(8,128)(2,1)S(1)}, u32[]{:S(2)}, u32[]{:S(2)}) collective-permute-start(bf16[400,128]{1,0:T(8,128)(2,1)S(1)} %sum_piece.7.refs_0_), channel_id=1, source_target_pairs={{0,12},{2,14},{4,0},{6,2},{8,4},{10,6},{12,8},{14,10},{1,13},{3,15... | collective-permute-start | bytes 307208 | tf_op jit(solution)/shard_map/ppermute | solution.py:49
  120.8 1.1 collective-permute-start.41
  121.9 1.9 %collective-permute-done.49.refs_4_ = bf16[400,128]{1,0:T(8,128)(2,1)S(1)} collective-permute-done((bf16[400,128]{1,0:T(8,128)(2,1)S(1)}, bf16[400,128]{1,0:T(8,128)(2,1)S(1)}, u32[]{:S(2)}, u32[]{:S(2)}) %collective-permute-start.49) | collective-permute-done | bytes 102432 | tf_op jit(solution)/shard_map/ppermute | solution.py:49
  123.7 4.4 %collective-permute-done.46.refs_2_ = bf16[400,128]{1,0:T(8,128)(2,1)S(1)} collective-permute-done((bf16[400,128]{1,0:T(8,128)(2,1)S(1)}, bf16[400,128]{1,0:T(8,128)(2,1)S(1)}, u32[]{:S(2)}, u32[]{:S(2)}) %collective-permute-start.46) | collective-permute-done | bytes 102432 | tf_op jit(solution)/shard_map/ppermute | solution.py:49
  128.3 2.5 %collective-permute-done.41.refs_6_ = bf16[400,128]{1,0:T(8,128)(2,1)S(1)} collective-permute-done((bf16[400,128]{1,0:T(8,128)(2,1)S(1)}, bf16[400,128]{1,0:T(8,128)(2,1)S(1)}, u32[]{:S(2)}, u32[]{:S(2)}) %collective-permute-start.41) | collective-permute-done | bytes 102432 | tf_op jit(solution)/shard_map/ppermute | solution.py:49
  130.8 1.1 collective-permute-start.47
  131.9 0.9 collective-permute-start.42
  133.4 3.0 %collective-permute-done.47.refs_2_ = bf16[400,128]{1,0:T(8,128)(2,1)S(1)} collective-permute-done((bf16[400,128]{1,0:T(8,128)(2,1)S(1)}, bf16[400,128]{1,0:T(8,128)(2,1)S(1)}, u32[]{:S(2)}, u32[]{:S(2)}) %collective-permute-start.47) | collective-permute-done | bytes 102432 | tf_op jit(solution)/shard_map/ppermute | solution.py:54
  136.4 1.1 collective-permute-done.42.refs_0_
  137.5 0.8 whole_partition.1
  138.3 1.3 relnew.3
  139.7 1.2 relnew.4
  140.9 1.5 %relnew.5 = (f32[400,2048]{1,0:T(8,128)}, f32[1,2048]{1,0:T(1,128)}) custom-call(f32[400,2048]{1,0:T(8,128)S(1)} %copy-done, f32[1,2048]{1,0:T(1,128)S(1)} %bitcast.29, bf16[400,128]{1,0:T(8,128)(2,1)S(1)} %collective-permute-done.42.refs_0_, bf16[400,128]{1,0:T(8,128)(2,1)S(1)} %collective-permute-done.43.refs_1_, ...), custom_call_target="tpu_custom_call", output_to_operand_aliasing={{0}: (4, {})} | custom-call | flops 409600 | bytes 409600 | tf_op jit(solution)/shard_map/relnew/pallas_call | solution.py:683
  (119 shorter events, 11.3 us)
Async XLA Ops:
  0.6 13.0 %copy-start.1 = (s32[6,4,128]{2,1,0:T(4,128)S(1)}, s32[6,4,128]{2,1,0:T(4,128)}, u32[]{:S(2)}) copy-start(s32[6,4,128]{2,1,0:T(4,128)} %ids_ref.25) | copy-start | bytes 36868
  5.9 10.7 %copy-start.2 = (s32[6,4,128]{2,1,0:T(4,128)S(1)}, s32[6,4,128]{2,1,0:T(4,128)}, u32[]{:S(2)}) copy-start(s32[6,4,128]{2,1,0:T(4,128)} %src_ref.11) | copy-start | bytes 36868
  5.9 10.7 %copy-start.3 = (s32[6,4,128]{2,1,0:T(4,128)S(1)}, s32[6,4,128]{2,1,0:T(4,128)}, u32[]{:S(2)}) copy-start(s32[6,4,128]{2,1,0:T(4,128)} %dst_ref.11) | copy-start | bytes 36868
  5.9 1.5 %collective-permute-start = (bf16[400,128]{1,0:T(8,128)(2,1)S(1)}, bf16[400,128]{1,0:T(8,128)(2,1)S(1)}, u32[]{:S(2)}, u32[]{:S(2)}) collective-permute-start(bf16[400,128]{1,0:T(8,128)(2,1)S(1)} %get-tuple-element.120), channel_id=1, source_target_pairs={{0,1},{1,0},{2,3},{3,2},{4,5},{5,4},{6,7},{7,6},{8,9},{9,8},{10,11... | collective-permute-start | bytes 307208 | tf_op jit(solution)/shard_map/ppermute | solution.py:58
  7.5 9.1 %collective-permute-start.2 = (bf16[400,128]{1,0:T(8,128)(2,1)S(1)}, bf16[400,128]{1,0:T(8,128)(2,1)S(1)}, u32[]{:S(2)}, u32[]{:S(2)}) collective-permute-start(bf16[400,128]{1,0:T(8,128)(2,1)S(1)} %get-tuple-element.123.own0), channel_id=1, source_target_pairs={{0,1},{1,0},{2,3},{3,2},{4,5},{5,4},{6,7},{7,6},{8,9},{9,8},{10,11... | collective-permute-start | bytes 307208 | tf_op jit(solution)/shard_map/ppermute | solution.py:58
  7.9 9.3 %collective-permute-start.1 = (bf16[400,128]{1,0:T(8,128)(2,1)S(1)}, bf16[400,128]{1,0:T(8,128)(2,1)S(1)}, u32[]{:S(2)}, u32[]{:S(2)}) collective-permute-start(bf16[400,128]{1,0:T(8,128)(2,1)S(1)} %get-tuple-element.123.own0), channel_id=1, source_target_pairs={{0,14},{2,0},{4,2},{6,4},{8,6},{10,8},{12,10},{14,12},{1,15},{3,1}... | collective-permute-start | bytes 307208 | tf_op jit(solution)/shard_map/ppermute | solution.py:49
  14.7 4.0 %copy-start.4 = (s32[6,4]{0,1:T(4,128)S(1)}, s32[6,4]{0,1:T(4,128)}, u32[]{:S(2)}) copy-start(s32[6,4]{0,1:T(4,128)} %param.16) | copy-start | bytes 292
  14.7 4.0 %copy-start.5 = (s32[6,4]{0,1:T(4,128)S(1)}, s32[6,4]{0,1:T(4,128)}, u32[]{:S(2)}) copy-start(s32[6,4]{0,1:T(4,128)} %param.17) | copy-start | bytes 292
  17.3 1.4 collective-permute-start.3
  20.2 1.4 collective-permute-start.4
  21.6 7.7 %collective-permute-start.5 = (bf16[400,128]{1,0:T(8,128)(2,1)S(1)}, bf16[400,128]{1,0:T(8,128)(2,1)S(1)}, u32[]{:S(2)}, u32[]{:S(2)}) collective-permute-start(bf16[400,128]{1,0:T(8,128)(2,1)S(1)} %sum_pair.9._), channel_id=1, source_target_pairs={{0,2},{2,4},{4,6},{6,8},{8,10},{10,12},{12,14},{14,0},{1,3},{3,5},... | collective-permute-start | bytes 307208 | tf_op jit(solution)/shard_map/ppermute | solution.py:49
  23.1 6.2 %collective-permute-start.6 = (bf16[400,128]{1,0:T(8,128)(2,1)S(1)}, bf16[400,128]{1,0:T(8,128)(2,1)S(1)}, u32[]{:S(2)}, u32[]{:S(2)}) collective-permute-start(bf16[400,128]{1,0:T(8,128)(2,1)S(1)} %get-tuple-element.138), channel_id=1, source_target_pairs={{0,1},{1,0},{2,3},{3,2},{4,5},{5,4},{6,7},{7,6},{8,9},{9,8},{10,11... | collective-permute-start | bytes 307208 | tf_op jit(solution)/shard_map/ppermute | solution.py:58
  29.5 2.4 %collective-permute-start.8 = (bf16[400,128]{1,0:T(8,128)(2,1)S(1)}, bf16[400,128]{1,0:T(8,128)(2,1)S(1)}, u32[]{:S(2)}, u32[]{:S(2)}) collective-permute-start(bf16[400,128]{1,0:T(8,128)(2,1)S(1)} %get-tuple-element.141.own0), channel_id=1, source_target_pairs={{0,1},{1,0},{2,3},{3,2},{4,5},{5,4},{6,7},{7,6},{8,9},{9,8},{10,11... | collective-permute-start | bytes 307208 | tf_op jit(solution)/shard_map/ppermute | solution.py:58
  29.5 5.3 %collective-permute-start.7 = (bf16[400,128]{1,0:T(8,128)(2,1)S(1)}, bf16[400,128]{1,0:T(8,128)(2,1)S(1)}, u32[]{:S(2)}, u32[]{:S(2)}) collective-permute-start(bf16[400,128]{1,0:T(8,128)(2,1)S(1)} %get-tuple-element.141.own0), channel_id=1, source_target_pairs={{0,12},{2,14},{4,0},{6,2},{8,4},{10,6},{12,8},{14,10},{1,13},{3,15... | collective-permute-start | bytes 307208 | tf_op jit(solution)/shard_map/ppermute | solution.py:49
  34.8 1.3 collective-permute-start.9
  37.7 1.4 collective-permute-start.10
  39.1 7.0 %collective-permute-start.11 = (bf16[400,128]{1,0:T(8,128)(2,1)S(1)}, bf16[400,128]{1,0:T(8,128)(2,1)S(1)}, u32[]{:S(2)}, u32[]{:S(2)}) collective-permute-start(bf16[400,128]{1,0:T(8,128)(2,1)S(1)} %sum_pair.11._), channel_id=1, source_target_pairs={{0,4},{2,6},{4,8},{6,10},{8,12},{10,14},{12,0},{14,2},{1,5},{3,7},... | collective-permute-start | bytes 307208 | tf_op jit(solution)/shard_map/ppermute | solution.py:49
  40.8 5.3 %collective-permute-start.12 = (bf16[400,128]{1,0:T(8,128)(2,1)S(1)}, bf16[400,128]{1,0:T(8,128)(2,1)S(1)}, u32[]{:S(2)}, u32[]{:S(2)}) collective-permute-start(bf16[400,128]{1,0:T(8,128)(2,1)S(1)} %get-tuple-element.155), channel_id=1, source_target_pairs={{0,1},{1,0},{2,3},{3,2},{4,5},{5,4},{6,7},{7,6},{8,9},{9,8},{10,11... | collective-permute-start | bytes 307208 | tf_op jit(solution)/shard_map/ppermute | solution.py:58
  46.2 2.4 %collective-permute-start.14 = (bf16[400,128]{1,0:T(8,128)(2,1)S(1)}, bf16[400,128]{1,0:T(8,128)(2,1)S(1)}, u32[]{:S(2)}, u32[]{:S(2)}) collective-permute-start(bf16[400,128]{1,0:T(8,128)(2,1)S(1)} %get-tuple-element.158.own0), channel_id=1, source_target_pairs={{0,1},{1,0},{2,3},{3,2},{4,5},{5,4},{6,7},{7,6},{8,9},{9,8},{10,11... | collective-permute-start | bytes 307208 | tf_op jit(solution)/shard_map/ppermute | solution.py:58
  46.3 6.2 %collective-permute-start.13 = (bf16[400,128]{1,0:T(8,128)(2,1)S(1)}, bf16[400,128]{1,0:T(8,128)(2,1)S(1)}, u32[]{:S(2)}, u32[]{:S(2)}) collective-permute-start(bf16[400,128]{1,0:T(8,128)(2,1)S(1)} %get-tuple-element.158.own0), channel_id=1, source_target_pairs={{0,10},{2,12},{4,14},{6,0},{8,2},{10,4},{12,6},{14,8},{1,11},{3,13... | collective-permute-start | bytes 307208 | tf_op jit(solution)/shard_map/ppermute | solution.py:49
  52.5 1.3 collective-permute-start.15
  55.4 1.4 collective-permute-start.16
  56.8 9.0 %collective-permute-start.17 = (bf16[400,128]{1,0:T(8,128)(2,1)S(1)}, bf16[400,128]{1,0:T(8,128)(2,1)S(1)}, u32[]{:S(2)}, u32[]{:S(2)}) collective-permute-start(bf16[400,128]{1,0:T(8,128)(2,1)S(1)} %sum_pair.13._), channel_id=1, source_target_pairs={{0,6},{2,8},{4,10},{6,12},{8,14},{10,0},{12,2},{14,4},{1,7},{3,9},... | collective-permute-start | bytes 307208 | tf_op jit(solution)/shard_map/ppermute | solution.py:49
  58.3 7.5 %collective-permute-start.18 = (bf16[400,128]{1,0:T(8,128)(2,1)S(1)}, bf16[400,128]{1,0:T(8,128)(2,1)S(1)}, u32[]{:S(2)}, u32[]{:S(2)}) collective-permute-start(bf16[400,128]{1,0:T(8,128)(2,1)S(1)} %get-tuple-element.172), channel_id=1, source_target_pairs={{0,1},{1,0},{2,3},{3,2},{4,5},{5,4},{6,7},{7,6},{8,9},{9,8},{10,11... | collective-permute-start | bytes 307208 | tf_op jit(solution)/shard_map/ppermute | solution.py:58
  65.9 2.4 %collective-permute-start.20 = (bf16[400,128]{1,0:T(8,128)(2,1)S(1)}, bf16[400,128]{1,0:T(8,128)(2,1)S(1)}, u32[]{:S(2)}, u32[]{:S(2)}) collective-permute-start(bf16[400,128]{1,0:T(8,128)(2,1)S(1)} %get-tuple-element.175.own0), channel_id=1, source_target_pairs={{0,1},{1,0},{2,3},{3,2},{4,5},{5,4},{6,7},{7,6},{8,9},{9,8},{10,11... | collective-permute-start | bytes 307208 | tf_op jit(solution)/shard_map/ppermute | solution.py:58
  66.0 7.0 %collective-permute-start.19 = (bf16[400,128]{1,0:T(8,128)(2,1)S(1)}, bf16[400,128]{1,0:T(8,128)(2,1)S(1)}, u32[]{:S(2)}, u32[]{:S(2)}) collective-permute-start(bf16[400,128]{1,0:T(8,128)(2,1)S(1)} %get-tuple-element.175.own0), channel_id=1, source_target_pairs={{0,8},{2,10},{4,12},{6,14},{8,0},{10,2},{12,4},{14,6},{1,9},{3,11}... | collective-permute-start | bytes 307208 | tf_op jit(solution)/shard_map/ppermute | solution.py:49
  73.0 1.3 collective-permute-start.21
  75.9 1.4 collective-permute-start.22
  77.3 7.8 %collective-permute-start.23 = (bf16[400,128]{1,0:T(8,128)(2,1)S(1)}, bf16[400,128]{1,0:T(8,128)(2,1)S(1)}, u32[]{:S(2)}, u32[]{:S(2)}) collective-permute-start(bf16[400,128]{1,0:T(8,128)(2,1)S(1)} %sum_pair.15._), channel_id=1, source_target_pairs={{0,8},{2,10},{4,12},{6,14},{8,0},{10,2},{12,4},{14,6},{1,9},{3,11}... | collective-permute-start | bytes 307208 | tf_op jit(solution)/shard_map/ppermute | solution.py:49
  78.9 6.3 %collective-permute-start.24 = (bf16[400,128]{1,0:T(8,128)(2,1)S(1)}, bf16[400,128]{1,0:T(8,128)(2,1)S(1)}, u32[]{:S(2)}, u32[]{:S(2)}) collective-permute-start(bf16[400,128]{1,0:T(8,128)(2,1)S(1)} %get-tuple-element.189), channel_id=1, source_target_pairs={{0,1},{1,0},{2,3},{3,2},{4,5},{5,4},{6,7},{7,6},{8,9},{9,8},{10,11... | collective-permute-start | bytes 307208 | tf_op jit(solution)/shard_map/ppermute | solution.py:58
  85.3 2.6 %collective-permute-start.26 = (bf16[400,128]{1,0:T(8,128)(2,1)S(1)}, bf16[400,128]{1,0:T(8,128)(2,1)S(1)}, u32[]{:S(2)}, u32[]{:S(2)}) collective-permute-start(bf16[400,128]{1,0:T(8,128)(2,1)S(1)} %get-tuple-element.192.own0), channel_id=1, source_target_pairs={{0,1},{1,0},{2,3},{3,2},{4,5},{5,4},{6,7},{7,6},{8,9},{9,8},{10,11... | collective-permute-start | bytes 307208 | tf_op jit(solution)/shard_map/ppermute | solution.py:58
  85.4 7.3 %collective-permute-start.25 = (bf16[400,128]{1,0:T(8,128)(2,1)S(1)}, bf16[400,128]{1,0:T(8,128)(2,1)S(1)}, u32[]{:S(2)}, u32[]{:S(2)}) collective-permute-start(bf16[400,128]{1,0:T(8,128)(2,1)S(1)} %get-tuple-element.192.own0), channel_id=1, source_target_pairs={{0,6},{2,8},{4,10},{6,12},{8,14},{10,0},{12,2},{14,4},{1,7},{3,9},... | collective-permute-start | bytes 307208 | tf_op jit(solution)/shard_map/ppermute | solution.py:49
  92.8 1.3 collective-permute-start.27
  96.2 1.4 collective-permute-start.29
  97.1 1.8 %collective-permute-start.32 = (bf16[4,400,128]{2,1,0:T(8,128)(2,1)S(1)}, bf16[4,400,128]{2,1,0:T(8,128)(2,1)S(1)}, u32[]{:S(2)}, u32[]{:S(2)}) collective-permute-start(bf16[4,400,128]{2,1,0:T(8,128)(2,1)S(1)} %get-tuple-element.213), channel_id=1, source_target_pairs={{0,1},{1,0},{2,3},{3,2},{4,5},{5,4},{6,7},{7,6},{8,9},{9,8},{10,11... | collective-permute-start | bytes 1228808 | tf_op jit(solution)/shard_map/ppermute | solution.py:58
  98.3 40.1 %copy-start = (f32[400,2048]{1,0:T(8,128)S(1)}, f32[400,2048]{1,0:T(8,128)}, u32[]{:S(2)}) copy-start(f32[400,2048]{1,0:T(8,128)} %rel_ref.7) | copy-start | bytes 9830404
  98.3 40.1 %copy-start.6 = (f32[2048]{0:T(1024)S(1)}, f32[2048]{0:T(1024)}, u32[]{:S(2)}) copy-start(f32[2048]{0:T(1024)} %param.12) | copy-start | bytes 24580
  98.3 2.9 %collective-permute-start.31 = (bf16[4,400,128]{2,1,0:T(8,128)(2,1)S(1)}, bf16[4,400,128]{2,1,0:T(8,128)(2,1)S(1)}, u32[]{:S(2)}, u32[]{:S(2)}) collective-permute-start(bf16[4,400,128]{2,1,0:T(8,128)(2,1)S(1)} %get-tuple-element.208), channel_id=1, source_target_pairs={{0,1},{1,0},{2,3},{3,2},{4,5},{5,4},{6,7},{7,6},{8,9},{9,8},{10,11... | collective-permute-start | bytes 1228808 | tf_op jit(solution)/shard_map/ppermute | solution.py:58
  99.0 6.0 %collective-permute-start.33 = (bf16[400,128]{1,0:T(8,128)(2,1)S(1)}, bf16[400,128]{1,0:T(8,128)(2,1)S(1)}, u32[]{:S(2)}, u32[]{:S(2)}) collective-permute-start(bf16[400,128]{1,0:T(8,128)(2,1)S(1)} %get-tuple-element.214), channel_id=1, source_target_pairs={{0,2},{2,0},{4,6},{6,4},{8,10},{10,8},{12,14},{14,12},{1,3},{3,1},... | collective-permute-start | bytes 307208 | tf_op jit(solution)/shard_map/ppermute | solution.py:54
  99.8 5.7 %collective-permute-start.28 = (bf16[400,128]{1,0:T(8,128)(2,1)S(1)}, bf16[400,128]{1,0:T(8,128)(2,1)S(1)}, u32[]{:S(2)}, u32[]{:S(2)}) collective-permute-start(bf16[400,128]{1,0:T(8,128)(2,1)S(1)} %get-tuple-element.203), channel_id=1, source_target_pairs={{0,1},{1,0},{2,3},{3,2},{4,5},{5,4},{6,7},{7,6},{8,9},{9,8},{10,11... | collective-permute-start | bytes 307208 | tf_op jit(solution)/shard_map/ppermute | solution.py:58
  99.9 9.2 %collective-permute-start.36 = (bf16[400,128]{1,0:T(8,128)(2,1)S(1)}, bf16[400,128]{1,0:T(8,128)(2,1)S(1)}, u32[]{:S(2)}, u32[]{:S(2)}) collective-permute-start(bf16[400,128]{1,0:T(8,128)(2,1)S(1)} %get-tuple-element.220), channel_id=1, source_target_pairs={{0,2},{2,0},{4,6},{6,4},{8,10},{10,8},{12,14},{14,12},{1,3},{3,1},... | collective-permute-start | bytes 307208 | tf_op jit(solution)/shard_map/ppermute | solution.py:54
  101.1 8.1 %collective-permute-start.30 = (bf16[400,128]{1,0:T(8,128)(2,1)S(1)}, bf16[400,128]{1,0:T(8,128)(2,1)S(1)}, u32[]{:S(2)}, u32[]{:S(2)}) collective-permute-start(bf16[400,128]{1,0:T(8,128)(2,1)S(1)} %sum_pair.17.refs_0_), channel_id=1, source_target_pairs={{0,10},{2,12},{4,14},{6,0},{8,2},{10,4},{12,6},{14,8},{1,11},{3,13... | collective-permute-start | bytes 307208 | tf_op jit(solution)/shard_map/ppermute | solution.py:49
  101.1 10.2 %collective-permute-start.38 = (bf16[400,128]{1,0:T(8,128)(2,1)S(1)}, bf16[400,128]{1,0:T(8,128)(2,1)S(1)}, u32[]{:S(2)}, u32[]{:S(2)}) collective-permute-start(bf16[400,128]{1,0:T(8,128)(2,1)S(1)} %get-tuple-element.222), channel_id=1, source_target_pairs={{0,2},{2,0},{4,6},{6,4},{8,10},{10,8},{12,14},{14,12},{1,3},{3,1},... | collective-permute-start | bytes 307208 | tf_op jit(solution)/shard_map/ppermute | solution.py:54
  105.0 9.0 %collective-permute-start.35 = (bf16[400,128]{1,0:T(8,128)(2,1)S(1)}, bf16[400,128]{1,0:T(8,128)(2,1)S(1)}, u32[]{:S(2)}, u32[]{:S(2)}) collective-permute-start(bf16[400,128]{1,0:T(8,128)(2,1)S(1)} %get-tuple-element.218), channel_id=1, source_target_pairs={{0,2},{2,0},{4,6},{6,4},{8,10},{10,8},{12,14},{14,12},{1,3},{3,1},... | collective-permute-start | bytes 307208 | tf_op jit(solution)/shard_map/ppermute | solution.py:54
  105.6 8.4 %collective-permute-start.40 = (bf16[400,128]{1,0:T(8,128)(2,1)S(1)}, bf16[400,128]{1,0:T(8,128)(2,1)S(1)}, u32[]{:S(2)}, u32[]{:S(2)}) collective-permute-start(bf16[400,128]{1,0:T(8,128)(2,1)S(1)} %sum_piece.4.refs_5_), channel_id=1, source_target_pairs={{0,4},{2,6},{4,8},{6,10},{8,12},{10,14},{12,0},{14,2},{1,5},{3,7},... | collective-permute-start | bytes 307208 | tf_op jit(solution)/shard_map/ppermute | solution.py:49
  109.2 7.1 %collective-permute-start.37 = (bf16[400,128]{1,0:T(8,128)(2,1)S(1)}, bf16[400,128]{1,0:T(8,128)(2,1)S(1)}, u32[]{:S(2)}, u32[]{:S(2)}) collective-permute-start(bf16[400,128]{1,0:T(8,128)(2,1)S(1)} %sum_piece.5), channel_id=1, source_target_pairs={{0,8},{2,10},{4,12},{6,14},{8,0},{10,2},{12,4},{14,6},{1,9},{3,11}... | collective-permute-start | bytes 307208 | tf_op jit(solution)/shard_map/ppermute | solution.py:49
  111.4 5.6 %collective-permute-start.39 = (bf16[400,128]{1,0:T(8,128)(2,1)S(1)}, bf16[400,128]{1,0:T(8,128)(2,1)S(1)}, u32[]{:S(2)}, u32[]{:S(2)}) collective-permute-start(bf16[400,128]{1,0:T(8,128)(2,1)S(1)} %sum_piece.6), channel_id=1, source_target_pairs={{0,12},{2,14},{4,0},{6,2},{8,4},{10,6},{12,8},{14,10},{1,13},{3,15... | collective-permute-start | bytes 307208 | tf_op jit(solution)/shard_map/ppermute | solution.py:49
  113.9 18.0 %collective-permute-start.34 = (f32[408,128]{1,0:T(8,128)S(1)}, f32[408,128]{1,0:T(8,128)S(1)}, u32[]{:S(2)}, u32[]{:S(2)}) collective-permute-start(f32[408,128]{1,0:T(8,128)S(1)} %update.11.mine), channel_id=1, source_target_pairs={{0,1},{1,0},{2,3},{3,2},{4,5},{5,4},{6,7},{7,6},{8,9},{9,8},{10,11... | collective-permute-start | bytes 626696 | tf_op jit(solution)/shard_map/ppermute | solution.py:58
  117.1 3.7 %collective-permute-start.52 = (bf16[400,128]{1,0:T(8,128)(2,1)S(1)}, bf16[400,128]{1,0:T(8,128)(2,1)S(1)}, u32[]{:S(2)}, u32[]{:S(2)}) collective-permute-start(bf16[400,128]{1,0:T(8,128)(2,1)S(1)} %sum_piece.7.refs_0_), channel_id=1, source_target_pairs={{0,1},{1,0},{2,3},{3,2},{4,5},{5,4},{6,7},{7,6},{8,9},{9,8},{10,11... | collective-permute-start | bytes 307208 | tf_op jit(solution)/shard_map/ppermute | solution.py:58
  117.1 6.6 %collective-permute-start.49 = (bf16[400,128]{1,0:T(8,128)(2,1)S(1)}, bf16[400,128]{1,0:T(8,128)(2,1)S(1)}, u32[]{:S(2)}, u32[]{:S(2)}) collective-permute-start(bf16[400,128]{1,0:T(8,128)(2,1)S(1)} %sum_piece.7.refs_0_), channel_id=1, source_target_pairs={{0,12},{2,14},{4,0},{6,2},{8,4},{10,6},{12,8},{14,10},{1,13},{3,15... | collective-permute-start | bytes 307208 | tf_op jit(solution)/shard_map/ppermute | solution.py:49
  120.5 7.6 %collective-permute-start.46 = (bf16[400,128]{1,0:T(8,128)(2,1)S(1)}, bf16[400,128]{1,0:T(8,128)(2,1)S(1)}, u32[]{:S(2)}, u32[]{:S(2)}) collective-permute-start(bf16[400,128]{1,0:T(8,128)(2,1)S(1)} %sum_piece.7.refs_0_), channel_id=1, source_target_pairs={{0,4},{2,6},{4,8},{6,10},{8,12},{10,14},{12,0},{14,2},{1,5},{3,7},... | collective-permute-start | bytes 307208 | tf_op jit(solution)/shard_map/ppermute | solution.py:49
  120.5 7.8 %collective-permute-start.44 = (bf16[400,128]{1,0:T(8,128)(2,1)S(1)}, bf16[400,128]{1,0:T(8,128)(2,1)S(1)}, u32[]{:S(2)}, u32[]{:S(2)}) collective-permute-start(bf16[400,128]{1,0:T(8,128)(2,1)S(1)} %sum_piece.7.refs_0_), channel_id=1, source_target_pairs={{0,2},{2,0},{4,6},{6,4},{8,10},{10,8},{12,14},{14,12},{1,3},{3,1},... | collective-permute-start | bytes 307208 | tf_op jit(solution)/shard_map/ppermute | solution.py:54
  120.8 10.0 %collective-permute-start.41 = (bf16[400,128]{1,0:T(8,128)(2,1)S(1)}, bf16[400,128]{1,0:T(8,128)(2,1)S(1)}, u32[]{:S(2)}, u32[]{:S(2)}) collective-permute-start(bf16[400,128]{1,0:T(8,128)(2,1)S(1)} %sum_piece.7.refs_0_), channel_id=1, source_target_pairs={{0,8},{2,10},{4,12},{6,14},{8,0},{10,2},{12,4},{14,6},{1,9},{3,11}... | collective-permute-start | bytes 307208 | tf_op jit(solution)/shard_map/ppermute | solution.py:49
  123.7 9.1 %collective-permute-start.54 = (bf16[400,128]{1,0:T(8,128)(2,1)S(1)}, bf16[400,128]{1,0:T(8,128)(2,1)S(1)}, u32[]{:S(2)}, u32[]{:S(2)}) collective-permute-start(bf16[400,128]{1,0:T(8,128)(2,1)S(1)} %collective-permute-done.49.refs_4_), channel_id=1, source_target_pairs={{0,1},{1,0},{2,3},{3,2},{4,5},{5,4},{6,7},{7,6},{8,9},{9,8},{10,11... | collective-permute-start | bytes 307208 | tf_op jit(solution)/shard_map/ppermute | solution.py:58
  128.1 4.7 %collective-permute-start.50 = (bf16[400,128]{1,0:T(8,128)(2,1)S(1)}, bf16[400,128]{1,0:T(8,128)(2,1)S(1)}, u32[]{:S(2)}, u32[]{:S(2)}) collective-permute-start(bf16[400,128]{1,0:T(8,128)(2,1)S(1)} %collective-permute-done.49.refs_4_), channel_id=1, source_target_pairs={{0,2},{2,0},{4,6},{6,4},{8,10},{10,8},{12,14},{14,12},{1,3},{3,1},... | collective-permute-start | bytes 307208 | tf_op jit(solution)/shard_map/ppermute | solution.py:54
  128.3 5.0 %collective-permute-start.53 = (bf16[400,128]{1,0:T(8,128)(2,1)S(1)}, bf16[400,128]{1,0:T(8,128)(2,1)S(1)}, u32[]{:S(2)}, u32[]{:S(2)}) collective-permute-start(bf16[400,128]{1,0:T(8,128)(2,1)S(1)} %collective-permute-done.46.refs_2_), channel_id=1, source_target_pairs={{0,1},{1,0},{2,3},{3,2},{4,5},{5,4},{6,7},{7,6},{8,9},{9,8},{10,11... | collective-permute-start | bytes 307208 | tf_op jit(solution)/shard_map/ppermute | solution.py:58
  130.8 5.6 %collective-permute-start.47 = (bf16[400,128]{1,0:T(8,128)(2,1)S(1)}, bf16[400,128]{1,0:T(8,128)(2,1)S(1)}, u32[]{:S(2)}, u32[]{:S(2)}) collective-permute-start(bf16[400,128]{1,0:T(8,128)(2,1)S(1)} %collective-permute-done.46.refs_2_), channel_id=1, source_target_pairs={{0,2},{2,0},{4,6},{6,4},{8,10},{10,8},{12,14},{14,12},{1,3},{3,1},... | collective-permute-start | bytes 307208 | tf_op jit(solution)/shard_map/ppermute | solution.py:54
  131.9 5.6 %collective-permute-start.42 = (bf16[400,128]{1,0:T(8,128)(2,1)S(1)}, bf16[400,128]{1,0:T(8,128)(2,1)S(1)}, u32[]{:S(2)}, u32[]{:S(2)}) collective-permute-start(bf16[400,128]{1,0:T(8,128)(2,1)S(1)} %collective-permute-done.41.refs_6_), channel_id=1, source_target_pairs={{0,2},{2,0},{4,6},{6,4},{8,10},{10,8},{12,14},{14,12},{1,3},{3,1},... | collective-permute-start | bytes 307208 | tf_op jit(solution)/shard_map/ppermute | solution.py:54
  132.8 5.5 %collective-permute-start.55 = (bf16[400,128]{1,0:T(8,128)(2,1)S(1)}, bf16[400,128]{1,0:T(8,128)(2,1)S(1)}, u32[]{:S(2)}, u32[]{:S(2)}) collective-permute-start(bf16[400,128]{1,0:T(8,128)(2,1)S(1)} %collective-permute-done.41.refs_6_), channel_id=1, source_target_pairs={{0,1},{1,0},{2,3},{3,2},{4,5},{5,4},{6,7},{7,6},{8,9},{9,8},{10,11... | collective-permute-start | bytes 307208 | tf_op jit(solution)/shard_map/ppermute | solution.py:58
  132.8 6.8 %collective-permute-start.45 = (bf16[400,128]{1,0:T(8,128)(2,1)S(1)}, bf16[400,128]{1,0:T(8,128)(2,1)S(1)}, u32[]{:S(2)}, u32[]{:S(2)}) collective-permute-start(bf16[400,128]{1,0:T(8,128)(2,1)S(1)} %collective-permute-done.44.refs_0_), channel_id=1, source_target_pairs={{0,1},{1,0},{2,3},{3,2},{4,5},{5,4},{6,7},{7,6},{8,9},{9,8},{10,11... | collective-permute-start | bytes 307208 | tf_op jit(solution)/shard_map/ppermute | solution.py:58
  133.4 6.3 %collective-permute-start.51 = (bf16[400,128]{1,0:T(8,128)(2,1)S(1)}, bf16[400,128]{1,0:T(8,128)(2,1)S(1)}, u32[]{:S(2)}, u32[]{:S(2)}) collective-permute-start(bf16[400,128]{1,0:T(8,128)(2,1)S(1)} %collective-permute-done.50.refs_4_), channel_id=1, source_target_pairs={{0,1},{1,0},{2,3},{3,2},{4,5},{5,4},{6,7},{7,6},{8,9},{9,8},{10,11... | collective-permute-start | bytes 307208 | tf_op jit(solution)/shard_map/ppermute | solution.py:58
  136.4 3.3 %collective-permute-start.48 = (bf16[400,128]{1,0:T(8,128)(2,1)S(1)}, bf16[400,128]{1,0:T(8,128)(2,1)S(1)}, u32[]{:S(2)}, u32[]{:S(2)}) collective-permute-start(bf16[400,128]{1,0:T(8,128)(2,1)S(1)} %collective-permute-done.47.refs_2_), channel_id=1, source_target_pairs={{0,1},{1,0},{2,3},{3,2},{4,5},{5,4},{6,7},{7,6},{8,9},{9,8},{10,11... | collective-permute-start | bytes 307208 | tf_op jit(solution)/shard_map/ppermute | solution.py:58
  137.5 3.4 %collective-permute-start.43 = (bf16[400,128]{1,0:T(8,128)(2,1)S(1)}, bf16[400,128]{1,0:T(8,128)(2,1)S(1)}, u32[]{:S(2)}, u32[]{:S(2)}) collective-permute-start(bf16[400,128]{1,0:T(8,128)(2,1)S(1)} %collective-permute-done.42.refs_0_), channel_id=1, source_target_pairs={{0,1},{1,0},{2,3},{3,2},{4,5},{5,4},{6,7},{7,6},{8,9},{9,8},{10,11... | collective-permute-start | bytes 307208 | tf_op jit(solution)/shard_map/ppermute | solution.py:58
where the time goes:
time: 143 us
  waiting for transfers between devices  67.5 us (47%)
  Pallas kernels  45.5 us (32%)
  starting transfers between devices  28 us (20%)
  between operations  1.49 us (1%)
    ppermute x16, waiting for transfers between devices, shifted(): return lax.ppermute(x, 'dom', [(i, (i + by) % n) for i in range(n)])  45.8 us
    ppermute x16, starting transfers between devices, shifted(): return lax.ppermute(x, 'dom', [(i, (i + by) % n) for i in range(n)])  14.1 us
    ppermute x32, waiting for transfers between devices, across(): return lax.ppermute(x, 'edge', [(0, 1), (1, 0)])  12.5 us
    pallas_call x5, Pallas kernels, relsum(): pl.pallas_call(functools.partial(relsum_kernel, t, acc is None), grid=(re...  10.7 us
    ppermute x8, waiting for transfers between devices, beside(): return lax.ppermute(x, 'dom', [(i, i ^ 1) for i in range(n)])  9.26 us
    ppermute x8, starting transfers between devices, beside(): return lax.ppermute(x, 'dom', [(i, i ^ 1) for i in range(n)])  9.01 us
    pallas_call x4, Pallas kernels, target_grad(): pl.pallas_call(functools.partial(target_kernel, t, shape), in_specs=[anyw...  6.26 us
    pallas_call x4, Pallas kernels, source_grad(): pl.pallas_call(functools.partial(source_grad_kernel, t, shape), in_specs=...  5.82 us
  transfers between devices with their start and end apart: 56, of which 29 were waited for; matrix products, arithmetic and copies ran while one was open for 0% of the time, Pallas kernels for 21%

commit v1 on v0

--- a/solution.py
+++ b/solution.py
@@ -655,17 +655,33 @@
     )(mine, theirs, *parts, *after)
 
 
+def stacked_kernel(*refs):
+    for i in range(refs[-1].shape[0]):
+        refs[-1][i] = refs[i][...]
+
+
+def stacked(parts, after):
+    return pl.pallas_call(
+        stacked_kernel,
+        in_specs=[vmem()] * len(parts) + [anywhere()] * len(after),
+        out_specs=vmem(),
+        out_shape=jax.ShapeDtypeStruct((len(parts), *parts[0].shape), parts[0].dtype),
+        compiler_params=params(),
+        name="stacked",
+    )(*parts, *after)
+
+
 def relnew_kernel(nz, same, ks, rel_ref, state_ref, *refs):
-    got = refs[: 2 * len(ks)]
+    mine, theirs = refs[: len(ks)], refs[len(ks)]
     rel_out, state_out, buf, sems = refs[-4:]
-    w = got[0].shape[1]
-    state_out[...] = refs[len(got) + (0 if same else 1)][...]
+    w = mine[0].shape[1]
+    state_out[...] = refs[len(ks) + (1 if same else 2)][...]
     z, x, edge = place()
     copies = []
-    for i, grad_ref in enumerate(got):
+    for i in range(2 * len(ks)):
         owner = 2 * lax.rem(z + nz - ks[i // 2], nz) + (x if same else 1 - x)
         at = pl.ds(first_column(owner, edge if i % 2 == 0 else 1 - edge, w), w)
-        grad = grad_ref[...].astype(F32)
+        grad = (mine[i // 2][...] if i % 2 == 0 else theirs[i // 2]).astype(F32)
         state = state_ref[:, at] + jnp.sum(grad * grad, axis=0, keepdims=True) / grad.shape[0]
         state_out[:, at] = state
         buf[i] = rel_ref[:, at] - grad * (learn_rate / jnp.sqrt(state))
@@ -676,23 +692,25 @@
         copy.wait()
 
 
-def relnew(nz, same, ks, relations, state, got, before, after):
+def relnew(nz, same, ks, relations, state, mine, theirs, before, after):
     dim, rels = relations.shape
-    w = got[0].shape[1]
+    w = mine[0].shape[1]
+    count = 2 * len(ks)
     start = [state] if before is None else list(before)
     return pl.pallas_call(
         functools.partial(relnew_kernel, nz, same, ks),
-        in_specs=[vmem()] * (2 + len(got)) + ([anywhere()] if before else [])
+        in_specs=[vmem()] * (3 + len(ks))
+        + ([anywhere()] if before else [])
         + [vmem()]
         + [anywhere()] * len(after),
         out_specs=[anywhere(), vmem()],
         out_shape=[jax.ShapeDtypeStruct((dim, rels), F32), jax.ShapeDtypeStruct((1, rels), F32)],
-        input_output_aliases={2 + len(got): 0} if before else {},
-        scratch_shapes=[pltpu.VMEM((len(got), dim, w), F32), pltpu.SemaphoreType.DMA((len(got),))],
-        compiler_params=params(),
-        cost_estimate=cost(4 * dim * w * len(got), 4 * dim * w * len(got)),
+        input_output_aliases={3 + len(ks): 0} if before else {},
+        scratch_shapes=[pltpu.VMEM((count, dim, w), F32), pltpu.SemaphoreType.DMA((count,))],
+        compiler_params=params(),
+        cost_estimate=cost(4 * dim * w * count, 4 * dim * w * count),
         name="relnew",
-    )(relations, state, *got, *start, *after)
+    )(relations, state, *mine, theirs, *start, *after)
 
 
 def relation_update(t, rel_ids, drel, acc, relations, state, gd_other, gd, grads, finish):
@@ -719,11 +737,12 @@
     got = [summed if k == 0 else shifted(summed, 2 * k) for k in range(nz)]
     got_x = [beside(piece) for piece in got]
     state = state.reshape(1, rels)
-    pairs = lambda ks, parts: [y for k in ks for y in (parts[k], across(parts[k]))]
-    early, late = near[:-1], near[-1:]
-    new = relnew(nz, True, near, relations, state, pairs(near, got), None, [done[2]])
-    new = relnew(nz, False, early, relations, state, pairs(early, got_x), new, [])
-    rel_new, state_new = relnew(nz, False, late, relations, state, pairs(late, got_x), new, [])
+    ks = near[:1] + near[:0:-1]
+    mine = [got[k] for k in ks]
+    new = relnew(nz, True, ks, relations, state, mine, across(stacked(mine, [done[2]])), None, [])
+    mine = [got_x[k] for k in ks]
+    theirs = across(stacked(mine, []))
+    rel_new, state_new = relnew(nz, False, ks, relations, state, mine, theirs, new, [])
     return rel_new, state_new.reshape(rels), done
 
 

time: 143 us -> 138 us (0.965)
  waiting for transfers between devices: 67.5 us -> 61.8 us
  starting transfers between devices: 28 us -> 29.5 us
    ppermute x16, waiting for transfers between devices: 45.8 us -> 41.7 us  [shifted(): return lax.ppermute(x, 'dom', [(i, (i + by) % n) for i in range(n)])]
    ppermute x8, starting transfers between devices: 9.01 us -> 11.7 us  [beside(): return lax.ppermute(x, 'dom', [(i, i ^ 1) for i in range(n)])]
    ppermute x8, waiting for transfers between devices: 9.26 us -> 7.21 us  [beside(): return lax.ppermute(x, 'dom', [(i, i ^ 1) for i in range(n)])]
    pallas_call x3 -> x2, Pallas kernels: 4 us -> 3.27 us  [relnew(): pl.pallas_call(functools.partial(relnew_kernel, nz, same, ks), in_specs=[...]
    ppermute x32 -> x26, starting transfers between devices: 4.88 us -> 4.33 us  [across(): return lax.ppermute(x, 'edge', [(0, 1), (1, 0)])]
    ppermute x32 -> x26, waiting for transfers between devices: 12.5 us -> 12.8 us  [across(): return lax.ppermute(x, 'edge', [(0, 1), (1, 0)])]
  transfers between devices with their start and end apart: 56 -> 50, of which waited for: 29 -> 28; matrix products, arithmetic and copies ran while one was open for 0% -> 0% of each run, Pallas kernels for 21% -> 21%
where the time goes in v1:
time: 138 us
  waiting for transfers between devices  61.8 us (45%)
  Pallas kernels  44.9 us (33%)
  starting transfers between devices  29.5 us (21%)
  between operations  1.48 us (1%)
    ppermute x16, waiting for transfers between devices, shifted(): return lax.ppermute(x, 'dom', [(i, (i + by) % n) for i in range(n)])  41.7 us
    ppermute x16, starting transfers between devices, shifted(): return lax.ppermute(x, 'dom', [(i, (i + by) % n) for i in range(n)])  13.6 us
    ppermute x26, waiting for transfers between devices, across(): return lax.ppermute(x, 'edge', [(0, 1), (1, 0)])  12.8 us
    ppermute x8, starting transfers between devices, beside(): return lax.ppermute(x, 'dom', [(i, i ^ 1) for i in range(n)])  11.7 us
    pallas_call x5, Pallas kernels, relsum(): pl.pallas_call(functools.partial(relsum_kernel, t, acc is None), grid=(re...  10.7 us
    ppermute x8, waiting for transfers between devices, beside(): return lax.ppermute(x, 'dom', [(i, i ^ 1) for i in range(n)])  7.21 us
    pallas_call x4, Pallas kernels, target_grad(): pl.pallas_call(functools.partial(target_kernel, t, shape), in_specs=[anyw...  6.27 us
    pallas_call x4, Pallas kernels, source_grad(): pl.pallas_call(functools.partial(source_grad_kernel, t, shape), in_specs=...  5.83 us
  transfers between devices with their start and end apart: 50, of which 28 were waited for; matrix products, arithmetic and copies ran while one was open for 0% of the time, Pallas kernels for 21%

profile of v1, /device:TPU:0, one launch (start us, length us, event | category | flops | bytes accessed | tf_op | source)
XLA Modules:
  0.0 137.7 jit_solution(11026010432802089966)
XLA Ops:
  0.6 5.3 %first_round.1 = (f32[400,128]{1,0:T(8,128)S(1)}, bf16[400,128]{1,0:T(8,128)(2,1)S(1)}, bf16[400,512]{1,0:T(8,128)(2,1)S(1)}, bf16[400,2048]{1,0:T(8,128)(2,1)S(...) custom-call(s32[4,6]{1,0:T(4,128)} %bitcast.6, s32[4,6]{1,0:T(4,128)} %bitcast.16, s32[6,4,128]{2,1,0:T(4,128)} %src_ref.11, ...), custom_call_target="tpu_custom_call" | custom-call | flops 1258291200 | bytes 6553600 | tf_op jit(solution)/shard_map/first_round/pallas_call | solution.py:299
  6.5 0.9 collective-permute-done.refs_3_
  8.0 5.7 %collective-permute-start.1 = (bf16[400,128]{1,0:T(8,128)(2,1)S(1)}, bf16[400,128]{1,0:T(8,128)(2,1)S(1)}, u32[]{:S(2)}, u32[]{:S(2)}) collective-permute-start(bf16[400,128]{1,0:T(8,128)(2,1)S(1)} %get-tuple-element.121.own0), channel_id=1, source_target_pairs={{0,14},{2,0},{4,2},{6,4},{8,6},{10,8},{12,10},{14,12},{1,15},{3,1}... | collective-permute-start | bytes 307208 | tf_op jit(solution)/shard_map/ppermute | solution.py:49
  13.6 1.0 relvec.5.rel_ref
  14.7 1.9 %relsum.5.refs_1_.refs_0_ = f32[400,2048]{1,0:T(8,128)S(1)} custom-call(s32[6,4,128]{2,1,0:T(4,128)S(1)} %copy-done.1, bf16[400,512]{1,0:T(8,128)(2,1)S(1)} %get-tuple-element.124.drel_ref), custom_call_target="tpu_custom_call" | custom-call | flops 204800 | bytes 204800 | tf_op jit(solution)/shard_map/relsum/pallas_call | solution.py:113
  16.6 0.6 source_side.5
  17.4 1.2 collective-permute-done.3.far1
  18.6 1.6 %target_grad.4 = (f32[400,128]{1,0:T(8,128)S(1)}, bf16[400,128]{1,0:T(8,128)(2,1)S(1)}, bf16[400,512]{1,0:T(8,128)(2,1)S(1)}, bf16[128,512]{1,0:T(8,128)(2,1)S(1)}, f32[1,512]{1,0:T(1,128)S(1)}) custom-call(s32[4,6]{1,0:T(4,128)S(1)} %bitcast.7, s32[4,6]{1,0:T(4,128)S(1)} %bitcast.17, bf16[400,128]{1,0:T(8,128)(2,1)S(1)} %held.5.far0, ...), custom_call_target="tpu_custom_call" | custom-call | flops 314572800 | bytes 2457600 | tf_op jit(solution)/shard_map/target_grad/pallas_call | solution.py:388
  20.4 1.2 collective-permute-done.4.b_ref
  21.7 1.5 %source_grad.4 = (f32[400,128]{1,0:T(8,128)S(1)}, bf16[400,128]{1,0:T(8,128)(2,1)S(1)}, bf16[400,512]{1,0:T(8,128)(2,1)S(1)}) custom-call(s32[4,6]{1,0:T(4,128)S(1)} %bitcast.8, s32[4,6]{1,0:T(4,128)S(1)} %bitcast.18, bf16[400,128]{1,0:T(8,128)(2,1)S(1)} %sum_pair.9._, bf16[400,512]{1,0:T(8,128)(2,1)S(1)} %get-tuple-element.130.o_ref, ...), custom_call_target="tpu_custom_call" | custom-call | flops 204800 | bytes 204800 | tf_op jit(solution)/shard_map/source_grad/pallas_call | solution.py:424
  23.3 1.0 relvec.6.refs_4_.rel_ref
  24.4 4.9 %collective-permute-done.5.b_ref = bf16[400,128]{1,0:T(8,128)(2,1)S(1)} collective-permute-done((bf16[400,128]{1,0:T(8,128)(2,1)S(1)}, bf16[400,128]{1,0:T(8,128)(2,1)S(1)}, u32[]{:S(2)}, u32[]{:S(2)}) %collective-permute-start.5) | collective-permute-done | bytes 102432 | tf_op jit(solution)/shard_map/ppermute | solution.py:49
  29.7 2.2 %relsum.6.refs_1_.refs_0_ = f32[400,2048]{1,0:T(8,128)S(1)} custom-call(s32[6,4,128]{2,1,0:T(4,128)S(1)} %copy-done.1, bf16[400,512]{1,0:T(8,128)(2,1)S(1)} %get-tuple-element.141.drel_ref, f32[400,2048]{1,0:T(8,128)S(1)} %relsum.5.refs_1_.refs_0_), custom_call_target="tpu_custom_call", output_to_operand_aliasing={{}: (2, {})} | custom-call | flops 204800 | bytes 204800 | tf_op jit(solution)/shard_map/relsum/pallas_call | solution.py:113
  32.5 2.4 %collective-permute-done.7.x_ref = bf16[400,128]{1,0:T(8,128)(2,1)S(1)} collective-permute-done((bf16[400,128]{1,0:T(8,128)(2,1)S(1)}, bf16[400,128]{1,0:T(8,128)(2,1)S(1)}, u32[]{:S(2)}, u32[]{:S(2)}) %collective-permute-start.7) | collective-permute-done | bytes 102432 | tf_op jit(solution)/shard_map/ppermute | solution.py:49
  34.8 1.3 collective-permute-done.9.far1
  36.1 1.6 %target_grad.5 = (f32[400,128]{1,0:T(8,128)S(1)}, bf16[400,128]{1,0:T(8,128)(2,1)S(1)}, bf16[400,512]{1,0:T(8,128)(2,1)S(1)}, bf16[128,512]{1,0:T(8,128)(2,1)S(1)}, f32[1,512]{1,0:T(1,128)S(1)}) custom-call(s32[4,6]{1,0:T(4,128)S(1)} %bitcast.9, s32[4,6]{1,0:T(4,128)S(1)} %bitcast.19, bf16[400,128]{1,0:T(8,128)(2,1)S(1)} %held.6.far0, ...), custom_call_target="tpu_custom_call" | custom-call | flops 314572800 | bytes 2457600 | tf_op jit(solution)/shard_map/target_grad/pallas_call | solution.py:388
  37.9 1.2 collective-permute-done.10.b_ref
  39.3 1.5 %source_grad.5 = (f32[400,128]{1,0:T(8,128)S(1)}, bf16[400,128]{1,0:T(8,128)(2,1)S(1)}, bf16[400,512]{1,0:T(8,128)(2,1)S(1)}) custom-call(s32[4,6]{1,0:T(4,128)S(1)} %bitcast.10, s32[4,6]{1,0:T(4,128)S(1)} %bitcast.20, bf16[400,128]{1,0:T(8,128)(2,1)S(1)} %sum_pair.11._, bf16[400,512]{1,0:T(8,128)(2,1)S(1)} %get-tuple-element.147.o_ref, ...), custom_call_target="tpu_custom_call" | custom-call | flops 204800 | bytes 204800 | tf_op jit(solution)/shard_map/source_grad/pallas_call | solution.py:424
  41.0 1.0 relvec.7.refs_4_.rel_ref
  42.1 4.0 %collective-permute-done.11.b_ref = bf16[400,128]{1,0:T(8,128)(2,1)S(1)} collective-permute-done((bf16[400,128]{1,0:T(8,128)(2,1)S(1)}, bf16[400,128]{1,0:T(8,128)(2,1)S(1)}, u32[]{:S(2)}, u32[]{:S(2)}) %collective-permute-start.11) | collective-permute-done | bytes 102432 | tf_op jit(solution)/shard_map/ppermute | solution.py:49
  46.4 2.2 %relsum.7.refs_1_.refs_0_ = f32[400,2048]{1,0:T(8,128)S(1)} custom-call(s32[6,4,128]{2,1,0:T(4,128)S(1)} %copy-done.1, bf16[400,512]{1,0:T(8,128)(2,1)S(1)} %get-tuple-element.158.drel_ref, f32[400,2048]{1,0:T(8,128)S(1)} %relsum.6.refs_1_.refs_0_), custom_call_target="tpu_custom_call", output_to_operand_aliasing={{}: (2, {})} | custom-call | flops 204800 | bytes 204800 | tf_op jit(solution)/shard_map/relsum/pallas_call | solution.py:113
  48.6 0.6 source_side.7
  49.2 3.3 %collective-permute-done.13.x_ref = bf16[400,128]{1,0:T(8,128)(2,1)S(1)} collective-permute-done((bf16[400,128]{1,0:T(8,128)(2,1)S(1)}, bf16[400,128]{1,0:T(8,128)(2,1)S(1)}, u32[]{:S(2)}, u32[]{:S(2)}) %collective-permute-start.13) | collective-permute-done | bytes 102432 | tf_op jit(solution)/shard_map/ppermute | solution.py:49
  52.5 1.3 collective-permute-done.15.far1
  53.8 1.6 %target_grad.6 = (f32[400,128]{1,0:T(8,128)S(1)}, bf16[400,128]{1,0:T(8,128)(2,1)S(1)}, bf16[400,512]{1,0:T(8,128)(2,1)S(1)}, bf16[128,512]{1,0:T(8,128)(2,1)S(1)}, f32[1,512]{1,0:T(1,128)S(1)}) custom-call(s32[4,6]{1,0:T(4,128)S(1)} %bitcast.11, s32[4,6]{1,0:T(4,128)S(1)} %bitcast.21, bf16[400,128]{1,0:T(8,128)(2,1)S(1)} %held.7.far0, ...), custom_call_target="tpu_custom_call" | custom-call | flops 314572800 | bytes 2457600 | tf_op jit(solution)/shard_map/target_grad/pallas_call | solution.py:388
  55.6 1.2 collective-permute-done.16.b_ref
  56.8 1.5 %source_grad.6 = (f32[400,128]{1,0:T(8,128)S(1)}, bf16[400,128]{1,0:T(8,128)(2,1)S(1)}, bf16[400,512]{1,0:T(8,128)(2,1)S(1)}) custom-call(s32[4,6]{1,0:T(4,128)S(1)} %bitcast.12, s32[4,6]{1,0:T(4,128)S(1)} %bitcast.22, bf16[400,128]{1,0:T(8,128)(2,1)S(1)} %sum_pair.13._, bf16[400,512]{1,0:T(8,128)(2,1)S(1)} %get-tuple-element.164.o_ref, ...), custom_call_target="tpu_custom_call" | custom-call | flops 204800 | bytes 204800 | tf_op jit(solution)/shard_map/source_grad/pallas_call | solution.py:424
  58.5 1.0 relvec.8.refs_4_.rel_ref
  59.6 6.2 %collective-permute-done.17.b_ref = bf16[400,128]{1,0:T(8,128)(2,1)S(1)} collective-permute-done((bf16[400,128]{1,0:T(8,128)(2,1)S(1)}, bf16[400,128]{1,0:T(8,128)(2,1)S(1)}, u32[]{:S(2)}, u32[]{:S(2)}) %collective-permute-start.17) | collective-permute-done | bytes 102432 | tf_op jit(solution)/shard_map/ppermute | solution.py:49
  66.1 2.2 %relsum.8.refs_1_.refs_0_ = f32[400,2048]{1,0:T(8,128)S(1)} custom-call(s32[6,4,128]{2,1,0:T(4,128)S(1)} %copy-done.1, bf16[400,512]{1,0:T(8,128)(2,1)S(1)} %get-tuple-element.175.drel_ref, f32[400,2048]{1,0:T(8,128)S(1)} %relsum.7.refs_1_.refs_0_), custom_call_target="tpu_custom_call", output_to_operand_aliasing={{}: (2, {})} | custom-call | flops 204800 | bytes 204800 | tf_op jit(solution)/shard_map/relsum/pallas_call | solution.py:113
  68.9 4.2 %collective-permute-done.19.x_ref = bf16[400,128]{1,0:T(8,128)(2,1)S(1)} collective-permute-done((bf16[400,128]{1,0:T(8,128)(2,1)S(1)}, bf16[400,128]{1,0:T(8,128)(2,1)S(1)}, u32[]{:S(2)}, u32[]{:S(2)}) %collective-permute-start.19) | collective-permute-done | bytes 102432 | tf_op jit(solution)/shard_map/ppermute | solution.py:49
  73.1 1.2 collective-permute-done.21.far1
  74.3 1.6 %target_grad.7 = (f32[400,128]{1,0:T(8,128)S(1)}, bf16[400,128]{1,0:T(8,128)(2,1)S(1)}, bf16[400,512]{1,0:T(8,128)(2,1)S(1)}, bf16[128,512]{1,0:T(8,128)(2,1)S(1)}, f32[1,512]{1,0:T(1,128)S(1)}) custom-call(s32[4,6]{1,0:T(4,128)S(1)} %bitcast.13, s32[4,6]{1,0:T(4,128)S(1)} %bitcast.23, bf16[400,128]{1,0:T(8,128)(2,1)S(1)} %held.8.far0, ...), custom_call_target="tpu_custom_call" | custom-call | flops 314572800 | bytes 2457600 | tf_op jit(solution)/shard_map/target_grad/pallas_call | solution.py:388
  76.1 1.2 collective-permute-done.22.b_ref
  77.4 1.5 %source_grad.7 = (f32[400,128]{1,0:T(8,128)S(1)}, bf16[400,128]{1,0:T(8,128)(2,1)S(1)}, bf16[400,512]{1,0:T(8,128)(2,1)S(1)}) custom-call(s32[4,6]{1,0:T(4,128)S(1)} %bitcast.14, s32[4,6]{1,0:T(4,128)S(1)} %bitcast.24, bf16[400,128]{1,0:T(8,128)(2,1)S(1)} %sum_pair.15._, bf16[400,512]{1,0:T(8,128)(2,1)S(1)} %get-tuple-element.181.o_ref, ...), custom_call_target="tpu_custom_call" | custom-call | flops 204800 | bytes 204800 | tf_op jit(solution)/shard_map/source_grad/pallas_call | solution.py:424
  79.1 1.0 relvec.9.refs_4_.rel_ref
  80.1 5.0 %collective-permute-done.23.b_ref = bf16[400,128]{1,0:T(8,128)(2,1)S(1)} collective-permute-done((bf16[400,128]{1,0:T(8,128)(2,1)S(1)}, bf16[400,128]{1,0:T(8,128)(2,1)S(1)}, u32[]{:S(2)}, u32[]{:S(2)}) %collective-permute-start.23) | collective-permute-done | bytes 102432 | tf_op jit(solution)/shard_map/ppermute | solution.py:49
  85.7 2.2 %relsum.9.refs_1_.acc_ref = f32[400,2048]{1,0:T(8,128)S(1)} custom-call(s32[6,4,128]{2,1,0:T(4,128)S(1)} %copy-done.1, bf16[400,512]{1,0:T(8,128)(2,1)S(1)} %get-tuple-element.192.drel_ref, f32[400,2048]{1,0:T(8,128)S(1)} %relsum.8.refs_1_.refs_0_), custom_call_target="tpu_custom_call", output_to_operand_aliasing={{}: (2, {})} | custom-call | flops 204800 | bytes 204800 | tf_op jit(solution)/shard_map/relsum/pallas_call | solution.py:113
  87.9 0.6 source_side.9
  88.5 4.3 %collective-permute-done.25.x_ref = bf16[400,128]{1,0:T(8,128)(2,1)S(1)} collective-permute-done((bf16[400,128]{1,0:T(8,128)(2,1)S(1)}, bf16[400,128]{1,0:T(8,128)(2,1)S(1)}, u32[]{:S(2)}, u32[]{:S(2)}) %collective-permute-start.25) | collective-permute-done | bytes 102432 | tf_op jit(solution)/shard_map/ppermute | solution.py:49
  92.8 1.3 collective-permute-done.27.far1
  94.1 1.7 %last_terms.1 = (bf16[400,512]{1,0:T(8,128)(2,1)S(1)}, bf16[400,512]{1,0:T(8,128)(2,1)S(1)}, bf16[400,512]{1,0:T(8,128)(2,1)S(1)}) custom-call(s32[4,6]{1,0:T(4,128)S(1)} %bitcast.15, s32[4,6]{1,0:T(4,128)S(1)} %bitcast.25, bf16[400,128]{1,0:T(8,128)(2,1)S(1)} %held.9.far0, bf16[400,128]{1,0:T(8,128)(2,1)S(1)} %collective-permute-done.27.far1, ...), custom_call_target="tpu_custom_call" | custom-call | flops 157286400 | bytes 2457600 | tf_op jit(solution)/shard_map/last_terms/pallas_call | solution.py:454
  96.4 0.7 pieces.3
  97.6 0.7 pieces.2
  99.0 0.8 collective-permute-start.33
  99.9 1.3 collective-permute-start.36
  101.2 3.8 %collective-permute-start.38 = (bf16[400,128]{1,0:T(8,128)(2,1)S(1)}, bf16[400,128]{1,0:T(8,128)(2,1)S(1)}, u32[]{:S(2)}, u32[]{:S(2)}) collective-permute-start(bf16[400,128]{1,0:T(8,128)(2,1)S(1)} %get-tuple-element.220), channel_id=1, source_target_pairs={{0,2},{2,0},{4,6},{6,4},{8,10},{10,8},{12,14},{14,12},{1,3},{3,1},... | collective-permute-start | bytes 307208 | tf_op jit(solution)/shard_map/ppermute | solution.py:54
  106.0 3.1 %collective-permute-done.36.refs_0_ = bf16[400,128]{1,0:T(8,128)(2,1)S(1)} collective-permute-done((bf16[400,128]{1,0:T(8,128)(2,1)S(1)}, bf16[400,128]{1,0:T(8,128)(2,1)S(1)}, u32[]{:S(2)}, u32[]{:S(2)}) %collective-permute-start.36) | collective-permute-done | bytes 102432 | tf_op jit(solution)/shard_map/ppermute | solution.py:54
  109.3 2.1 %collective-permute-done.38.refs_0_ = bf16[400,128]{1,0:T(8,128)(2,1)S(1)} collective-permute-done((bf16[400,128]{1,0:T(8,128)(2,1)S(1)}, bf16[400,128]{1,0:T(8,128)(2,1)S(1)}, u32[]{:S(2)}, u32[]{:S(2)}) %collective-permute-start.38) | collective-permute-done | bytes 102432 | tf_op jit(solution)/shard_map/ppermute | solution.py:54
  111.4 2.4 %collective-permute-start.39 = (bf16[400,128]{1,0:T(8,128)(2,1)S(1)}, bf16[400,128]{1,0:T(8,128)(2,1)S(1)}, u32[]{:S(2)}, u32[]{:S(2)}) collective-permute-start(bf16[400,128]{1,0:T(8,128)(2,1)S(1)} %sum_piece.6), channel_id=1, source_target_pairs={{0,12},{2,14},{4,0},{6,2},{8,4},{10,6},{12,8},{14,10},{1,13},{3,15... | collective-permute-start | bytes 307208 | tf_op jit(solution)/shard_map/ppermute | solution.py:49
  114.0 2.2 %collective-permute-done.37.refs_1_ = bf16[400,128]{1,0:T(8,128)(2,1)S(1)} collective-permute-done((bf16[400,128]{1,0:T(8,128)(2,1)S(1)}, bf16[400,128]{1,0:T(8,128)(2,1)S(1)}, u32[]{:S(2)}, u32[]{:S(2)}) %collective-permute-start.37) | collective-permute-done | bytes 102432 | tf_op jit(solution)/shard_map/ppermute | solution.py:49
  116.2 0.7 collective-permute-done.39.refs_2_
  117.1 1.5 %collective-permute-start.46 = (bf16[400,128]{1,0:T(8,128)(2,1)S(1)}, bf16[400,128]{1,0:T(8,128)(2,1)S(1)}, u32[]{:S(2)}, u32[]{:S(2)}) collective-permute-start(bf16[400,128]{1,0:T(8,128)(2,1)S(1)} %sum_piece.7.refs_0_), channel_id=1, source_target_pairs={{0,4},{2,6},{4,8},{6,10},{8,12},{10,14},{12,0},{14,2},{1,5},{3,7},... | collective-permute-start | bytes 307208 | tf_op jit(solution)/shard_map/ppermute | solution.py:49
  118.6 2.3 %collective-permute-start.44 = (bf16[400,128]{1,0:T(8,128)(2,1)S(1)}, bf16[400,128]{1,0:T(8,128)(2,1)S(1)}, u32[]{:S(2)}, u32[]{:S(2)}) collective-permute-start(bf16[400,128]{1,0:T(8,128)(2,1)S(1)} %sum_piece.7.refs_0_), channel_id=1, source_target_pairs={{0,12},{2,14},{4,0},{6,2},{8,4},{10,6},{12,8},{14,10},{1,13},{3,15... | collective-permute-start | bytes 307208 | tf_op jit(solution)/shard_map/ppermute | solution.py:49
  121.0 1.5 %collective-permute-start.41 = (bf16[400,128]{1,0:T(8,128)(2,1)S(1)}, bf16[400,128]{1,0:T(8,128)(2,1)S(1)}, u32[]{:S(2)}, u32[]{:S(2)}) collective-permute-start(bf16[400,128]{1,0:T(8,128)(2,1)S(1)} %sum_piece.7.refs_0_), channel_id=1, source_target_pairs={{0,2},{2,0},{4,6},{6,4},{8,10},{10,8},{12,14},{14,12},{1,3},{3,1},... | collective-permute-start | bytes 307208 | tf_op jit(solution)/shard_map/ppermute | solution.py:54
  122.5 2.2 %collective-permute-done.46.refs_3_ = bf16[400,128]{1,0:T(8,128)(2,1)S(1)} collective-permute-done((bf16[400,128]{1,0:T(8,128)(2,1)S(1)}, bf16[400,128]{1,0:T(8,128)(2,1)S(1)}, u32[]{:S(2)}, u32[]{:S(2)}) %collective-permute-start.46) | collective-permute-done | bytes 102432 | tf_op jit(solution)/shard_map/ppermute | solution.py:49
  124.7 1.3 collective-permute-start.47
  125.9 0.8 collective-permute-start.45
  126.7 2.4 %collective-permute-done.42.refs_1_ = bf16[400,128]{1,0:T(8,128)(2,1)S(1)} collective-permute-done((bf16[400,128]{1,0:T(8,128)(2,1)S(1)}, bf16[400,128]{1,0:T(8,128)(2,1)S(1)}, u32[]{:S(2)}, u32[]{:S(2)}) %collective-permute-start.42) | collective-permute-done | bytes 102432 | tf_op jit(solution)/shard_map/ppermute | solution.py:49
  129.1 1.7 %collective-permute-start.43 = (bf16[400,128]{1,0:T(8,128)(2,1)S(1)}, bf16[400,128]{1,0:T(8,128)(2,1)S(1)}, u32[]{:S(2)}, u32[]{:S(2)}) collective-permute-start(bf16[400,128]{1,0:T(8,128)(2,1)S(1)} %collective-permute-done.42.refs_1_), channel_id=1, source_target_pairs={{0,2},{2,0},{4,6},{6,4},{8,10},{10,8},{12,14},{14,12},{1,3},{3,1},... | collective-permute-start | bytes 307208 | tf_op jit(solution)/shard_map/ppermute | solution.py:54
  130.7 0.8 whole_partition.1
  131.7 2.0 %collective-permute-done.43.refs_1_ = bf16[400,128]{1,0:T(8,128)(2,1)S(1)} collective-permute-done((bf16[400,128]{1,0:T(8,128)(2,1)S(1)}, bf16[400,128]{1,0:T(8,128)(2,1)S(1)}, u32[]{:S(2)}, u32[]{:S(2)}) %collective-permute-start.43) | collective-permute-done | bytes 102432 | tf_op jit(solution)/shard_map/ppermute | solution.py:54
  133.9 1.3 relnew.2
  135.6 1.9 %relnew.3 = (f32[400,2048]{1,0:T(8,128)}, f32[1,2048]{1,0:T(1,128)}) custom-call(f32[400,2048]{1,0:T(8,128)S(1)} %copy-done, f32[1,2048]{1,0:T(1,128)S(1)} %bitcast.28, bf16[400,128]{1,0:T(8,128)(2,1)S(1)} %collective-permute-done.41.refs_0_, bf16[400,128]{1,0:T(8,128)(2,1)S(1)} %collective-permute-done.43.refs_1_, ...), custom_call_target="tpu_custom_call", output_to_operand_aliasing={{0}: (7, {})} | custom-call | flops 1638400 | bytes 1638400 | tf_op jit(solution)/shard_map/relnew/pallas_call | solution.py:700
  (108 shorter events, 10.1 us)
Async XLA Ops:
  0.6 13.0 %copy-start.1 = (s32[6,4,128]{2,1,0:T(4,128)S(1)}, s32[6,4,128]{2,1,0:T(4,128)}, u32[]{:S(2)}) copy-start(s32[6,4,128]{2,1,0:T(4,128)} %ids_ref.25) | copy-start | bytes 36868
  5.9 10.7 %copy-start.2 = (s32[6,4,128]{2,1,0:T(4,128)S(1)}, s32[6,4,128]{2,1,0:T(4,128)}, u32[]{:S(2)}) copy-start(s32[6,4,128]{2,1,0:T(4,128)} %src_ref.11) | copy-start | bytes 36868
  5.9 10.7 %copy-start.3 = (s32[6,4,128]{2,1,0:T(4,128)S(1)}, s32[6,4,128]{2,1,0:T(4,128)}, u32[]{:S(2)}) copy-start(s32[6,4,128]{2,1,0:T(4,128)} %dst_ref.11) | copy-start | bytes 36868
  5.9 1.5 %collective-permute-start = (bf16[400,128]{1,0:T(8,128)(2,1)S(1)}, bf16[400,128]{1,0:T(8,128)(2,1)S(1)}, u32[]{:S(2)}, u32[]{:S(2)}) collective-permute-start(bf16[400,128]{1,0:T(8,128)(2,1)S(1)} %get-tuple-element.118), channel_id=1, source_target_pairs={{0,1},{1,0},{2,3},{3,2},{4,5},{5,4},{6,7},{7,6},{8,9},{9,8},{10,11... | collective-permute-start | bytes 307208 | tf_op jit(solution)/shard_map/ppermute | solution.py:58
  7.5 9.1 %collective-permute-start.2 = (bf16[400,128]{1,0:T(8,128)(2,1)S(1)}, bf16[400,128]{1,0:T(8,128)(2,1)S(1)}, u32[]{:S(2)}, u32[]{:S(2)}) collective-permute-start(bf16[400,128]{1,0:T(8,128)(2,1)S(1)} %get-tuple-element.121.own0), channel_id=1, source_target_pairs={{0,1},{1,0},{2,3},{3,2},{4,5},{5,4},{6,7},{7,6},{8,9},{9,8},{10,11... | collective-permute-start | bytes 307208 | tf_op jit(solution)/shard_map/ppermute | solution.py:58
  8.0 9.3 %collective-permute-start.1 = (bf16[400,128]{1,0:T(8,128)(2,1)S(1)}, bf16[400,128]{1,0:T(8,128)(2,1)S(1)}, u32[]{:S(2)}, u32[]{:S(2)}) collective-permute-start(bf16[400,128]{1,0:T(8,128)(2,1)S(1)} %get-tuple-element.121.own0), channel_id=1, source_target_pairs={{0,14},{2,0},{4,2},{6,4},{8,6},{10,8},{12,10},{14,12},{1,15},{3,1}... | collective-permute-start | bytes 307208 | tf_op jit(solution)/shard_map/ppermute | solution.py:49
  14.7 4.0 %copy-start.4 = (s32[6,4]{0,1:T(4,128)S(1)}, s32[6,4]{0,1:T(4,128)}, u32[]{:S(2)}) copy-start(s32[6,4]{0,1:T(4,128)} %param.16) | copy-start | bytes 292
  14.7 4.0 %copy-start.5 = (s32[6,4]{0,1:T(4,128)S(1)}, s32[6,4]{0,1:T(4,128)}, u32[]{:S(2)}) copy-start(s32[6,4]{0,1:T(4,128)} %param.17) | copy-start | bytes 292
  17.3 1.4 collective-permute-start.3
  20.2 1.4 collective-permute-start.4
  21.6 7.7 %collective-permute-start.5 = (bf16[400,128]{1,0:T(8,128)(2,1)S(1)}, bf16[400,128]{1,0:T(8,128)(2,1)S(1)}, u32[]{:S(2)}, u32[]{:S(2)}) collective-permute-start(bf16[400,128]{1,0:T(8,128)(2,1)S(1)} %sum_pair.9._), channel_id=1, source_target_pairs={{0,2},{2,4},{4,6},{6,8},{8,10},{10,12},{12,14},{14,0},{1,3},{3,5},... | collective-permute-start | bytes 307208 | tf_op jit(solution)/shard_map/ppermute | solution.py:49
  23.1 6.2 %collective-permute-start.6 = (bf16[400,128]{1,0:T(8,128)(2,1)S(1)}, bf16[400,128]{1,0:T(8,128)(2,1)S(1)}, u32[]{:S(2)}, u32[]{:S(2)}) collective-permute-start(bf16[400,128]{1,0:T(8,128)(2,1)S(1)} %get-tuple-element.136), channel_id=1, source_target_pairs={{0,1},{1,0},{2,3},{3,2},{4,5},{5,4},{6,7},{7,6},{8,9},{9,8},{10,11... | collective-permute-start | bytes 307208 | tf_op jit(solution)/shard_map/ppermute | solution.py:58
  29.4 2.4 %collective-permute-start.8 = (bf16[400,128]{1,0:T(8,128)(2,1)S(1)}, bf16[400,128]{1,0:T(8,128)(2,1)S(1)}, u32[]{:S(2)}, u32[]{:S(2)}) collective-permute-start(bf16[400,128]{1,0:T(8,128)(2,1)S(1)} %get-tuple-element.139.own0), channel_id=1, source_target_pairs={{0,1},{1,0},{2,3},{3,2},{4,5},{5,4},{6,7},{7,6},{8,9},{9,8},{10,11... | collective-permute-start | bytes 307208 | tf_op jit(solution)/shard_map/ppermute | solution.py:58
  29.5 5.3 %collective-permute-start.7 = (bf16[400,128]{1,0:T(8,128)(2,1)S(1)}, bf16[400,128]{1,0:T(8,128)(2,1)S(1)}, u32[]{:S(2)}, u32[]{:S(2)}) collective-permute-start(bf16[400,128]{1,0:T(8,128)(2,1)S(1)} %get-tuple-element.139.own0), channel_id=1, source_target_pairs={{0,12},{2,14},{4,0},{6,2},{8,4},{10,6},{12,8},{14,10},{1,13},{3,15... | collective-permute-start | bytes 307208 | tf_op jit(solution)/shard_map/ppermute | solution.py:49
  34.8 1.3 collective-permute-start.9
  37.7 1.4 collective-permute-start.10
  39.1 7.0 %collective-permute-start.11 = (bf16[400,128]{1,0:T(8,128)(2,1)S(1)}, bf16[400,128]{1,0:T(8,128)(2,1)S(1)}, u32[]{:S(2)}, u32[]{:S(2)}) collective-permute-start(bf16[400,128]{1,0:T(8,128)(2,1)S(1)} %sum_pair.11._), channel_id=1, source_target_pairs={{0,4},{2,6},{4,8},{6,10},{8,12},{10,14},{12,0},{14,2},{1,5},{3,7},... | collective-permute-start | bytes 307208 | tf_op jit(solution)/shard_map/ppermute | solution.py:49
  40.8 5.3 %collective-permute-start.12 = (bf16[400,128]{1,0:T(8,128)(2,1)S(1)}, bf16[400,128]{1,0:T(8,128)(2,1)S(1)}, u32[]{:S(2)}, u32[]{:S(2)}) collective-permute-start(bf16[400,128]{1,0:T(8,128)(2,1)S(1)} %get-tuple-element.153), channel_id=1, source_target_pairs={{0,1},{1,0},{2,3},{3,2},{4,5},{5,4},{6,7},{7,6},{8,9},{9,8},{10,11... | collective-permute-start | bytes 307208 | tf_op jit(solution)/shard_map/ppermute | solution.py:58
  46.2 2.4 %collective-permute-start.14 = (bf16[400,128]{1,0:T(8,128)(2,1)S(1)}, bf16[400,128]{1,0:T(8,128)(2,1)S(1)}, u32[]{:S(2)}, u32[]{:S(2)}) collective-permute-start(bf16[400,128]{1,0:T(8,128)(2,1)S(1)} %get-tuple-element.156.own0), channel_id=1, source_target_pairs={{0,1},{1,0},{2,3},{3,2},{4,5},{5,4},{6,7},{7,6},{8,9},{9,8},{10,11... | collective-permute-start | bytes 307208 | tf_op jit(solution)/shard_map/ppermute | solution.py:58
  46.3 6.2 %collective-permute-start.13 = (bf16[400,128]{1,0:T(8,128)(2,1)S(1)}, bf16[400,128]{1,0:T(8,128)(2,1)S(1)}, u32[]{:S(2)}, u32[]{:S(2)}) collective-permute-start(bf16[400,128]{1,0:T(8,128)(2,1)S(1)} %get-tuple-element.156.own0), channel_id=1, source_target_pairs={{0,10},{2,12},{4,14},{6,0},{8,2},{10,4},{12,6},{14,8},{1,11},{3,13... | collective-permute-start | bytes 307208 | tf_op jit(solution)/shard_map/ppermute | solution.py:49
  52.5 1.3 collective-permute-start.15
  55.4 1.4 collective-permute-start.16
  56.8 9.0 %collective-permute-start.17 = (bf16[400,128]{1,0:T(8,128)(2,1)S(1)}, bf16[400,128]{1,0:T(8,128)(2,1)S(1)}, u32[]{:S(2)}, u32[]{:S(2)}) collective-permute-start(bf16[400,128]{1,0:T(8,128)(2,1)S(1)} %sum_pair.13._), channel_id=1, source_target_pairs={{0,6},{2,8},{4,10},{6,12},{8,14},{10,0},{12,2},{14,4},{1,7},{3,9},... | collective-permute-start | bytes 307208 | tf_op jit(solution)/shard_map/ppermute | solution.py:49
  58.3 7.5 %collective-permute-start.18 = (bf16[400,128]{1,0:T(8,128)(2,1)S(1)}, bf16[400,128]{1,0:T(8,128)(2,1)S(1)}, u32[]{:S(2)}, u32[]{:S(2)}) collective-permute-start(bf16[400,128]{1,0:T(8,128)(2,1)S(1)} %get-tuple-element.170), channel_id=1, source_target_pairs={{0,1},{1,0},{2,3},{3,2},{4,5},{5,4},{6,7},{7,6},{8,9},{9,8},{10,11... | collective-permute-start | bytes 307208 | tf_op jit(solution)/shard_map/ppermute | solution.py:58
  65.9 2.4 %collective-permute-start.20 = (bf16[400,128]{1,0:T(8,128)(2,1)S(1)}, bf16[400,128]{1,0:T(8,128)(2,1)S(1)}, u32[]{:S(2)}, u32[]{:S(2)}) collective-permute-start(bf16[400,128]{1,0:T(8,128)(2,1)S(1)} %get-tuple-element.173.own0), channel_id=1, source_target_pairs={{0,1},{1,0},{2,3},{3,2},{4,5},{5,4},{6,7},{7,6},{8,9},{9,8},{10,11... | collective-permute-start | bytes 307208 | tf_op jit(solution)/shard_map/ppermute | solution.py:58
  66.0 7.0 %collective-permute-start.19 = (bf16[400,128]{1,0:T(8,128)(2,1)S(1)}, bf16[400,128]{1,0:T(8,128)(2,1)S(1)}, u32[]{:S(2)}, u32[]{:S(2)}) collective-permute-start(bf16[400,128]{1,0:T(8,128)(2,1)S(1)} %get-tuple-element.173.own0), channel_id=1, source_target_pairs={{0,8},{2,10},{4,12},{6,14},{8,0},{10,2},{12,4},{14,6},{1,9},{3,11}... | collective-permute-start | bytes 307208 | tf_op jit(solution)/shard_map/ppermute | solution.py:49
  73.0 1.3 collective-permute-start.21
  75.9 1.4 collective-permute-start.22
  77.3 7.8 %collective-permute-start.23 = (bf16[400,128]{1,0:T(8,128)(2,1)S(1)}, bf16[400,128]{1,0:T(8,128)(2,1)S(1)}, u32[]{:S(2)}, u32[]{:S(2)}) collective-permute-start(bf16[400,128]{1,0:T(8,128)(2,1)S(1)} %sum_pair.15._), channel_id=1, source_target_pairs={{0,8},{2,10},{4,12},{6,14},{8,0},{10,2},{12,4},{14,6},{1,9},{3,11}... | collective-permute-start | bytes 307208 | tf_op jit(solution)/shard_map/ppermute | solution.py:49
  78.9 6.3 %collective-permute-start.24 = (bf16[400,128]{1,0:T(8,128)(2,1)S(1)}, bf16[400,128]{1,0:T(8,128)(2,1)S(1)}, u32[]{:S(2)}, u32[]{:S(2)}) collective-permute-start(bf16[400,128]{1,0:T(8,128)(2,1)S(1)} %get-tuple-element.187), channel_id=1, source_target_pairs={{0,1},{1,0},{2,3},{3,2},{4,5},{5,4},{6,7},{7,6},{8,9},{9,8},{10,11... | collective-permute-start | bytes 307208 | tf_op jit(solution)/shard_map/ppermute | solution.py:58
  85.3 2.6 %collective-permute-start.26 = (bf16[400,128]{1,0:T(8,128)(2,1)S(1)}, bf16[400,128]{1,0:T(8,128)(2,1)S(1)}, u32[]{:S(2)}, u32[]{:S(2)}) collective-permute-start(bf16[400,128]{1,0:T(8,128)(2,1)S(1)} %get-tuple-element.190.own0), channel_id=1, source_target_pairs={{0,1},{1,0},{2,3},{3,2},{4,5},{5,4},{6,7},{7,6},{8,9},{9,8},{10,11... | collective-permute-start | bytes 307208 | tf_op jit(solution)/shard_map/ppermute | solution.py:58
  85.4 7.3 %collective-permute-start.25 = (bf16[400,128]{1,0:T(8,128)(2,1)S(1)}, bf16[400,128]{1,0:T(8,128)(2,1)S(1)}, u32[]{:S(2)}, u32[]{:S(2)}) collective-permute-start(bf16[400,128]{1,0:T(8,128)(2,1)S(1)} %get-tuple-element.190.own0), channel_id=1, source_target_pairs={{0,6},{2,8},{4,10},{6,12},{8,14},{10,0},{12,2},{14,4},{1,7},{3,9},... | collective-permute-start | bytes 307208 | tf_op jit(solution)/shard_map/ppermute | solution.py:49
  92.7 1.3 collective-permute-start.27
  96.2 1.4 collective-permute-start.29
  97.1 1.8 %collective-permute-start.32 = (bf16[4,400,128]{2,1,0:T(8,128)(2,1)S(1)}, bf16[4,400,128]{2,1,0:T(8,128)(2,1)S(1)}, u32[]{:S(2)}, u32[]{:S(2)}) collective-permute-start(bf16[4,400,128]{2,1,0:T(8,128)(2,1)S(1)} %get-tuple-element.211), channel_id=1, source_target_pairs={{0,1},{1,0},{2,3},{3,2},{4,5},{5,4},{6,7},{7,6},{8,9},{9,8},{10,11... | collective-permute-start | bytes 1228808 | tf_op jit(solution)/shard_map/ppermute | solution.py:58
  98.3 2.9 %collective-permute-start.31 = (bf16[4,400,128]{2,1,0:T(8,128)(2,1)S(1)}, bf16[4,400,128]{2,1,0:T(8,128)(2,1)S(1)}, u32[]{:S(2)}, u32[]{:S(2)}) collective-permute-start(bf16[4,400,128]{2,1,0:T(8,128)(2,1)S(1)} %get-tuple-element.206), channel_id=1, source_target_pairs={{0,1},{1,0},{2,3},{3,2},{4,5},{5,4},{6,7},{7,6},{8,9},{9,8},{10,11... | collective-permute-start | bytes 1228808 | tf_op jit(solution)/shard_map/ppermute | solution.py:58
  99.0 6.0 %collective-permute-start.33 = (bf16[400,128]{1,0:T(8,128)(2,1)S(1)}, bf16[400,128]{1,0:T(8,128)(2,1)S(1)}, u32[]{:S(2)}, u32[]{:S(2)}) collective-permute-start(bf16[400,128]{1,0:T(8,128)(2,1)S(1)} %get-tuple-element.212), channel_id=1, source_target_pairs={{0,2},{2,0},{4,6},{6,4},{8,10},{10,8},{12,14},{14,12},{1,3},{3,1},... | collective-permute-start | bytes 307208 | tf_op jit(solution)/shard_map/ppermute | solution.py:54
  99.8 5.7 %collective-permute-start.28 = (bf16[400,128]{1,0:T(8,128)(2,1)S(1)}, bf16[400,128]{1,0:T(8,128)(2,1)S(1)}, u32[]{:S(2)}, u32[]{:S(2)}) collective-permute-start(bf16[400,128]{1,0:T(8,128)(2,1)S(1)} %get-tuple-element.201), channel_id=1, source_target_pairs={{0,1},{1,0},{2,3},{3,2},{4,5},{5,4},{6,7},{7,6},{8,9},{9,8},{10,11... | collective-permute-start | bytes 307208 | tf_op jit(solution)/shard_map/ppermute | solution.py:58
  99.9 9.3 %collective-permute-start.36 = (bf16[400,128]{1,0:T(8,128)(2,1)S(1)}, bf16[400,128]{1,0:T(8,128)(2,1)S(1)}, u32[]{:S(2)}, u32[]{:S(2)}) collective-permute-start(bf16[400,128]{1,0:T(8,128)(2,1)S(1)} %get-tuple-element.218), channel_id=1, source_target_pairs={{0,2},{2,0},{4,6},{6,4},{8,10},{10,8},{12,14},{14,12},{1,3},{3,1},... | collective-permute-start | bytes 307208 | tf_op jit(solution)/shard_map/ppermute | solution.py:54
  101.1 8.1 %collective-permute-start.30 = (bf16[400,128]{1,0:T(8,128)(2,1)S(1)}, bf16[400,128]{1,0:T(8,128)(2,1)S(1)}, u32[]{:S(2)}, u32[]{:S(2)}) collective-permute-start(bf16[400,128]{1,0:T(8,128)(2,1)S(1)} %sum_pair.17.refs_0_), channel_id=1, source_target_pairs={{0,10},{2,12},{4,14},{6,0},{8,2},{10,4},{12,6},{14,8},{1,11},{3,13... | collective-permute-start | bytes 307208 | tf_op jit(solution)/shard_map/ppermute | solution.py:49
  101.2 10.2 %collective-permute-start.38 = (bf16[400,128]{1,0:T(8,128)(2,1)S(1)}, bf16[400,128]{1,0:T(8,128)(2,1)S(1)}, u32[]{:S(2)}, u32[]{:S(2)}) collective-permute-start(bf16[400,128]{1,0:T(8,128)(2,1)S(1)} %get-tuple-element.220), channel_id=1, source_target_pairs={{0,2},{2,0},{4,6},{6,4},{8,10},{10,8},{12,14},{14,12},{1,3},{3,1},... | collective-permute-start | bytes 307208 | tf_op jit(solution)/shard_map/ppermute | solution.py:54
  105.0 9.0 %collective-permute-start.35 = (bf16[400,128]{1,0:T(8,128)(2,1)S(1)}, bf16[400,128]{1,0:T(8,128)(2,1)S(1)}, u32[]{:S(2)}, u32[]{:S(2)}) collective-permute-start(bf16[400,128]{1,0:T(8,128)(2,1)S(1)} %get-tuple-element.216), channel_id=1, source_target_pairs={{0,2},{2,0},{4,6},{6,4},{8,10},{10,8},{12,14},{14,12},{1,3},{3,1},... | collective-permute-start | bytes 307208 | tf_op jit(solution)/shard_map/ppermute | solution.py:54
  105.5 28.4 %copy-start = (f32[400,2048]{1,0:T(8,128)S(1)}, f32[400,2048]{1,0:T(8,128)}, u32[]{:S(2)}) copy-start(f32[400,2048]{1,0:T(8,128)} %rel_ref.5) | copy-start | bytes 9830404
  105.5 28.4 %copy-start.6 = (f32[2048]{0:T(1024)S(1)}, f32[2048]{0:T(1024)}, u32[]{:S(2)}) copy-start(f32[2048]{0:T(1024)} %param.12) | copy-start | bytes 24580
  105.6 8.4 %collective-permute-start.40 = (bf16[400,128]{1,0:T(8,128)(2,1)S(1)}, bf16[400,128]{1,0:T(8,128)(2,1)S(1)}, u32[]{:S(2)}, u32[]{:S(2)}) collective-permute-start(bf16[400,128]{1,0:T(8,128)(2,1)S(1)} %sum_piece.4.refs_5_), channel_id=1, source_target_pairs={{0,4},{2,6},{4,8},{6,10},{8,12},{10,14},{12,0},{14,2},{1,5},{3,7},... | collective-permute-start | bytes 307208 | tf_op jit(solution)/shard_map/ppermute | solution.py:49
  109.2 7.1 %collective-permute-start.37 = (bf16[400,128]{1,0:T(8,128)(2,1)S(1)}, bf16[400,128]{1,0:T(8,128)(2,1)S(1)}, u32[]{:S(2)}, u32[]{:S(2)}) collective-permute-start(bf16[400,128]{1,0:T(8,128)(2,1)S(1)} %sum_piece.5), channel_id=1, source_target_pairs={{0,8},{2,10},{4,12},{6,14},{8,0},{10,2},{12,4},{14,6},{1,9},{3,11}... | collective-permute-start | bytes 307208 | tf_op jit(solution)/shard_map/ppermute | solution.py:49
  111.4 5.6 %collective-permute-start.39 = (bf16[400,128]{1,0:T(8,128)(2,1)S(1)}, bf16[400,128]{1,0:T(8,128)(2,1)S(1)}, u32[]{:S(2)}, u32[]{:S(2)}) collective-permute-start(bf16[400,128]{1,0:T(8,128)(2,1)S(1)} %sum_piece.6), channel_id=1, source_target_pairs={{0,12},{2,14},{4,0},{6,2},{8,4},{10,6},{12,8},{14,10},{1,13},{3,15... | collective-permute-start | bytes 307208 | tf_op jit(solution)/shard_map/ppermute | solution.py:49
  113.9 16.8 %collective-permute-start.34 = (f32[408,128]{1,0:T(8,128)S(1)}, f32[408,128]{1,0:T(8,128)S(1)}, u32[]{:S(2)}, u32[]{:S(2)}) collective-permute-start(f32[408,128]{1,0:T(8,128)S(1)} %update.11.mine), channel_id=1, source_target_pairs={{0,1},{1,0},{2,3},{3,2},{4,5},{5,4},{6,7},{7,6},{8,9},{9,8},{10,11... | collective-permute-start | bytes 626696 | tf_op jit(solution)/shard_map/ppermute | solution.py:58
  117.1 7.6 %collective-permute-start.46 = (bf16[400,128]{1,0:T(8,128)(2,1)S(1)}, bf16[400,128]{1,0:T(8,128)(2,1)S(1)}, u32[]{:S(2)}, u32[]{:S(2)}) collective-permute-start(bf16[400,128]{1,0:T(8,128)(2,1)S(1)} %sum_piece.7.refs_0_), channel_id=1, source_target_pairs={{0,4},{2,6},{4,8},{6,10},{8,12},{10,14},{12,0},{14,2},{1,5},{3,7},... | collective-permute-start | bytes 307208 | tf_op jit(solution)/shard_map/ppermute | solution.py:49
  118.6 7.3 %collective-permute-start.44 = (bf16[400,128]{1,0:T(8,128)(2,1)S(1)}, bf16[400,128]{1,0:T(8,128)(2,1)S(1)}, u32[]{:S(2)}, u32[]{:S(2)}) collective-permute-start(bf16[400,128]{1,0:T(8,128)(2,1)S(1)} %sum_piece.7.refs_0_), channel_id=1, source_target_pairs={{0,12},{2,14},{4,0},{6,2},{8,4},{10,6},{12,8},{14,10},{1,13},{3,15... | collective-permute-start | bytes 307208 | tf_op jit(solution)/shard_map/ppermute | solution.py:49
  121.0 8.1 %collective-permute-start.42 = (bf16[400,128]{1,0:T(8,128)(2,1)S(1)}, bf16[400,128]{1,0:T(8,128)(2,1)S(1)}, u32[]{:S(2)}, u32[]{:S(2)}) collective-permute-start(bf16[400,128]{1,0:T(8,128)(2,1)S(1)} %sum_piece.7.refs_0_), channel_id=1, source_target_pairs={{0,8},{2,10},{4,12},{6,14},{8,0},{10,2},{12,4},{14,6},{1,9},{3,11}... | collective-permute-start | bytes 307208 | tf_op jit(solution)/shard_map/ppermute | solution.py:49
  121.0 10.7 %collective-permute-start.41 = (bf16[400,128]{1,0:T(8,128)(2,1)S(1)}, bf16[400,128]{1,0:T(8,128)(2,1)S(1)}, u32[]{:S(2)}, u32[]{:S(2)}) collective-permute-start(bf16[400,128]{1,0:T(8,128)(2,1)S(1)} %sum_piece.7.refs_0_), channel_id=1, source_target_pairs={{0,2},{2,0},{4,6},{6,4},{8,10},{10,8},{12,14},{14,12},{1,3},{3,1},... | collective-permute-start | bytes 307208 | tf_op jit(solution)/shard_map/ppermute | solution.py:54
  124.7 7.0 %collective-permute-start.47 = (bf16[400,128]{1,0:T(8,128)(2,1)S(1)}, bf16[400,128]{1,0:T(8,128)(2,1)S(1)}, u32[]{:S(2)}, u32[]{:S(2)}) collective-permute-start(bf16[400,128]{1,0:T(8,128)(2,1)S(1)} %collective-permute-done.46.refs_3_), channel_id=1, source_target_pairs={{0,2},{2,0},{4,6},{6,4},{8,10},{10,8},{12,14},{14,12},{1,3},{3,1},... | collective-permute-start | bytes 307208 | tf_op jit(solution)/shard_map/ppermute | solution.py:54
  125.9 5.8 %collective-permute-start.45 = (bf16[400,128]{1,0:T(8,128)(2,1)S(1)}, bf16[400,128]{1,0:T(8,128)(2,1)S(1)}, u32[]{:S(2)}, u32[]{:S(2)}) collective-permute-start(bf16[400,128]{1,0:T(8,128)(2,1)S(1)} %collective-permute-done.44.refs_2_), channel_id=1, source_target_pairs={{0,2},{2,0},{4,6},{6,4},{8,10},{10,8},{12,14},{14,12},{1,3},{3,1},... | collective-permute-start | bytes 307208 | tf_op jit(solution)/shard_map/ppermute | solution.py:54
  129.1 4.7 %collective-permute-start.43 = (bf16[400,128]{1,0:T(8,128)(2,1)S(1)}, bf16[400,128]{1,0:T(8,128)(2,1)S(1)}, u32[]{:S(2)}, u32[]{:S(2)}) collective-permute-start(bf16[400,128]{1,0:T(8,128)(2,1)S(1)} %collective-permute-done.42.refs_1_), channel_id=1, source_target_pairs={{0,2},{2,0},{4,6},{6,4},{8,10},{10,8},{12,14},{14,12},{1,3},{3,1},... | collective-permute-start | bytes 307208 | tf_op jit(solution)/shard_map/ppermute | solution.py:54
  131.6 2.3 %collective-permute-start.49 = (bf16[4,400,128]{2,1,0:T(8,128)(2,1)S(1)}, bf16[4,400,128]{2,1,0:T(8,128)(2,1)S(1)}, u32[]{:S(2)}, u32[]{:S(2)}) collective-permute-start(bf16[4,400,128]{2,1,0:T(8,128)(2,1)S(1)} %stacked.3), channel_id=1, source_target_pairs={{0,1},{1,0},{2,3},{3,2},{4,5},{5,4},{6,7},{7,6},{8,9},{9,8},{10,11... | collective-permute-start | bytes 1228808 | tf_op jit(solution)/shard_map/ppermute | solution.py:58
  133.8 1.8 %collective-permute-start.48 = (bf16[4,400,128]{2,1,0:T(8,128)(2,1)S(1)}, bf16[4,400,128]{2,1,0:T(8,128)(2,1)S(1)}, u32[]{:S(2)}, u32[]{:S(2)}) collective-permute-start(bf16[4,400,128]{2,1,0:T(8,128)(2,1)S(1)} %stacked.2), channel_id=1, source_target_pairs={{0,1},{1,0},{2,3},{3,2},{4,5},{5,4},{6,7},{7,6},{8,9},{9,8},{10,11... | collective-permute-start | bytes 1228808 | tf_op jit(solution)/shard_map/ppermute | solution.py:58
